TPU v7x, 128 devices: a whole 4x4x4 slice. The times are simulated.
128 devices in a mesh: dp: 8 (over y_lo, x), axial: 16 (over z, y_hi, core).
Axes of the slice: x: 4, y: 4 (y_hi: 2, y_lo: 2; y = y_hi * 2 + y_lo), z: 4, core: 2. Of those that a mesh axis runs over, the one named last changes fastest.
Arguments:
- pair: bfloat16 [8, 256, 256, 128], P('dp', 'axial'), may hold values from -6 to 6
- cotangent: bfloat16 [8, 256, 256, 128], P('dp', 'axial'), may hold values from -6 to 6
- in_weight: bfloat16 [128, 640], replicated, may hold values from -0.5 to 0.5
- out_weight: bfloat16 [128, 128], replicated, may hold values from -0.5 to 0.5
- gain_in: float32 [128], replicated, may hold values from 0.5 to 1.5
- gain_x: float32 [128], replicated, may hold values from 0.5 to 1.5
Outputs:
- updated: bfloat16 [8, 256, 256, 128], P('dp', 'axial')
- grad_pair: bfloat16 [8, 256, 256, 128], P('dp', 'axial')
- grad_in_weight: float32 [128, 640], replicated
- grad_out_weight: float32 [128, 128], replicated
- grad_gain_in: float32 [128], replicated
- grad_gain_x: float32 [128], replicated
All inputs are finite; a program needn't handle non-finite values.
Results may differ from a plain program's by a relative error of at most 0.015.
Values may be sent and summed in bfloat16 or wider, within the bound.
A program may use at most 192 MiB of HBM per device.

v0:
```python
import jax
import jax.numpy as jnp
from jax import lax
from jax.sharding import PartitionSpec as P


def norm_stats(values, gain):
    center = jnp.mean(values, axis=-1, keepdims=True)
    shifted = values - center
    spread = jnp.sqrt(jnp.mean(shifted * shifted, axis=-1, keepdims=True) + 1e-05)
    unit_val = shifted / spread
    return (unit_val * gain, unit_val, spread)


def norm_back(grad_norm, unit_val, spread, gain):
    scaled = grad_norm * gain
    mean_one = jnp.mean(scaled, axis=-1, keepdims=True)
    mean_two = jnp.mean(scaled * unit_val, axis=-1, keepdims=True)
    return (scaled - mean_one - unit_val * mean_two) / spread


def local(pair, cotangent, in_weight, out_weight, gain_in, gain_x):
    pair_rows = pair[0]
    upstream = cotangent[0].astype(jnp.float32)
    rows, width, chan = pair_rows.shape
    hidden = out_weight.shape[0]
    normed, unit_in, spread_in = norm_stats(pair_rows.astype(jnp.float32), gain_in)
    normed = normed.astype(jnp.bfloat16)
    flat_in = normed.reshape(rows * width, chan)
    projected = jnp.dot(flat_in, in_weight, preferred_element_type=jnp.float32).reshape(
        rows, width, -1
    )
    proj_a = projected[..., :hidden]
    gate_a = jax.nn.sigmoid(projected[..., hidden : 2 * hidden])
    proj_b = projected[..., 2 * hidden : 3 * hidden]
    gate_b = jax.nn.sigmoid(projected[..., 3 * hidden : 4 * hidden])
    gate_out = jax.nn.sigmoid(projected[..., 4 * hidden :])
    left = (gate_a * proj_a).astype(jnp.bfloat16)
    right = (gate_b * proj_b).astype(jnp.bfloat16)
    product = jnp.einsum(
        "ikc,jkc->ijc",
        left,
        lax.all_gather(right, "axial", axis=0, tiled=True),
        preferred_element_type=jnp.float32,
    )
    xnorm, unit_x, spread_x = norm_stats(product, gain_x)
    xnorm = xnorm.astype(jnp.bfloat16)
    flat_x = xnorm.reshape(rows * width, hidden)
    lifted = jnp.dot(flat_x, out_weight, preferred_element_type=jnp.float32).reshape(
        rows, width, chan
    )
    updated = (gate_out * lifted).astype(jnp.bfloat16)
    grad_lift = (upstream * gate_out).astype(jnp.bfloat16)
    grad_gate = upstream * lifted * gate_out * (1.0 - gate_out)
    flat_lift = grad_lift.reshape(rows * width, chan)
    local_out = jnp.dot(flat_x.T, flat_lift, preferred_element_type=jnp.float32)
    grad_xnorm = jnp.dot(flat_lift, out_weight.T, preferred_element_type=jnp.float32).reshape(
        rows, width, hidden
    )
    local_gx = jnp.sum(grad_xnorm * unit_x, axis=(0, 1))
    grad_prod = norm_back(grad_xnorm, unit_x, spread_x, gain_x).astype(jnp.bfloat16)
    sub_grad = grad_prod
    grad_left = jnp.einsum(
        "ijc,jkc->ikc",
        sub_grad,
        lax.all_gather(right, "axial", axis=0, tiled=True),
        preferred_element_type=jnp.float32,
    )
    sub_grad = grad_prod
    grad_right = lax.psum_scatter(
        jnp.einsum("ijc,ikc->jkc", sub_grad, left, preferred_element_type=jnp.float32).astype(
            jnp.bfloat16
        ),
        "axial",
        scatter_dimension=0,
        tiled=True,
    ).astype(jnp.float32)
    grad_proj = jnp.concatenate(
        [
            grad_left * gate_a,
            grad_left * proj_a * gate_a * (1.0 - gate_a),
            grad_right * gate_b,
            grad_right * proj_b * gate_b * (1.0 - gate_b),
            grad_gate,
        ],
        axis=-1,
    ).astype(jnp.bfloat16)
    flat_proj = grad_proj.reshape(rows * width, -1)
    local_in = jnp.dot(flat_in.T, flat_proj, preferred_element_type=jnp.float32)
    grad_normed = jnp.dot(flat_proj, in_weight.T, preferred_element_type=jnp.float32).reshape(
        rows, width, chan
    )
    local_gi = jnp.sum(grad_normed * unit_in, axis=(0, 1))
    grad_pair = norm_back(grad_normed, unit_in, spread_in, gain_in).astype(jnp.bfloat16)
    totals = lax.psum((local_in, local_out, local_gi, local_gx), ("dp", "axial"))
    factor = 1.0 / jnp.sqrt(jnp.float32(lax.axis_size("dp") * width * width))
    return (
        updated[None],
        grad_pair[None],
        totals[0] * factor,
        totals[1] * factor,
        totals[2] * factor,
        totals[3] * factor,
    )


def solution(mesh):
    in_specs = (P("dp", "axial", None, None), P("dp", "axial", None, None), P(), P(), P(), P())
    out_specs = (P("dp", "axial", None, None), P("dp", "axial", None, None), P(), P(), P(), P())
    return jax.shard_map(local, mesh=mesh, in_specs=in_specs, out_specs=out_specs, check_vma=False)
```

profile of v0, /device:TPU:1, one launch (start us, length us, event | category | flops | bytes accessed | tf_op | source)
XLA Modules:
  0.0 586.1 jit_solution(8048160565218089413)
XLA Ops:
  7.2 1.5 copy.28
  9.3 1.6 fusion.39
  10.9 2.7 multiply_convert_fusion.2
  13.7 1.5 copy-done.1
  15.4 1.7 copy.31
  17.1 3.7 fusion.41
  20.8 107.5 %all-gather.2.cloned.1.call-done = bf16[256,256,128]{2,1,0:T(8,128)(2,1)} async-done(((bf16[16,256,128]{2,1,0:T(8,128)(2,1)}), bf16[256,256,128]{2,1,0:T(8,128)(2,1)}) %all-gather.2.cloned.1.call-update) | async-done | bytes 16777232 | tf_op jit(solution)/shard_map/all_gather | solution.py:43
  128.4 22.1 %copy.30 = bf16[256,256,128]{1,0,2:T(8,128)(2,1)} copy(bf16[256,256,128]{2,1,0:T(8,128)(2,1)} %all-gather.2.cloned.1.call-done) | data formatting | bytes 33554432 | tf_op jit(solution)/shard_map/all_gather | solution.py:43
  150.5 8.4 %bitcast_reduce_fusion = (f32[16,256]{1,0:T(8,128)S(1)}, f32[128,256,16]{1,2,0:T(8,128)S(1)}) fusion(bf16[256,256,128]{1,0,2:T(8,128)(2,1)} %copy.30, bf16[16,256,128]{1,0,2:T(8,128)(2,1)} %copy.31), kind=kOutput, calls=%fused_computation.38 | convolution fusion | flops 268955648 | bytes 19939328 | tf_op jit(solution)/shard_map/ikc,jkc->ijc/dot_general | solution.py:40
  159.2 1.3 copy-done.2
  160.5 3.1 multiply_reduce_fusion
  163.6 12.2 %fusion.50 = bf16[128,256,256]{2,1,0:T(8,128)(2,1)} fusion(bf16[16,256,128]{1,0,2:T(8,128)(2,1)} %copy.31, f32[16,256,128]{1,2,0:T(8,128)} %fusion.41, f32[16,256]{1,0:T(8,128)S(1)} %get-tuple-element.36, f32[16,256]{1,0:T(8,128)S(1)} %get-tuple-element.37, f32[128]{0:T(128)S(1)} %copy-done.7, f32[16,256]{1,0:T(8,128)S(1)} %add_sqrt_fusion, ...), kind=kOutput, calls=%fused_computation.86 | convolution fusion | flops 272629760 | bytes 22086144 | tf_op jit(solution)/shard_map/ijc,ikc->jkc/dot_general | solution.py:71
  175.8 24.3 %copy.39 = bf16[128,256,256]{0,1,2:T(8,128)(2,1)} copy(bf16[128,256,256]{2,1,0:T(8,128)(2,1)} %fusion.50) | data formatting | bytes 33554432 | tf_op jit(solution)/shard_map/ijc,ikc->jkc/dot_general | solution.py:71
  200.4 11.2 %fusion.51 = f32[128,256,16]{1,2,0:T(8,128)} fusion(bf16[256,256,128]{1,0,2:T(8,128)(2,1)} %copy.30, f32[16,256,128]{1,2,0:T(8,128)} %fusion.41, f32[16,256]{1,0:T(8,128)S(1)} %get-tuple-element.36, f32[16,256]{1,0:T(8,128)S(1)} %get-tuple-element.37, f32[128]{0:T(128)S(1)} %copy-done.7, f32[16,256]{1,0:T(8,128)S(1)} %add_sqrt_fusion, ...), kind=kOutput, calls=%fused_computation.87 | convolution fusion | flops 272629760 | bytes 23134720 | tf_op jit(solution)/shard_map/ijc,jkc->ikc/dot_general | solution.py:63
  211.7 2.3 copy.37
  214.0 3.8 fusion.29
  217.8 3.6 convolution_bitcast_fusion.1
  221.4 4.7 fusion.28
  226.1 117.5 %reduce-scatter.2.cloned.1.call-done = bf16[16,256,128]{2,1,0:T(8,128)(2,1)} async-done(((bf16[256,256,128]{2,1,0:T(8,128)(2,1)}), bf16[16,256,128]{2,1,0:T(8,128)(2,1)}) %reduce-scatter.2.cloned.1.call-update) | async-done | bytes 1048592 | tf_op jit(solution)/shard_map/reduce_scatter | solution.py:70
  343.6 3.6 fusion.32
  347.2 4.2 fusion.31
  351.4 3.8 fusion.30
  355.2 5.7 multiply_reduce_fusion.1
  360.9 4.3 convolution_bitcast_fusion
  365.1 3.3 fusion.27
  368.4 0.8 fusion.33
  369.2 1.3 copy.43
  370.5 64.4 %all-reduce = (f32[128]{0:T(128)S(1)}, f32[128]{0:T(128)S(1)}) all-reduce(f32[128]{0:T(128)S(1)} %get-tuple-element.20, f32[128]{0:T(128)S(1)} %get-tuple-element.18), channel_id=1, replica_groups=mesh['dp'=8,'axial'=16] {'dp','axial'}, use_global_device_ids=true, to_apply=%region_12.0 | all-reduce | flops 256 | bytes 2048 | tf_op jit(solution)/shard_map/psum | solution.py:95
  435.4 0.5 broadcast_multiply_fusion.8
  435.9 140.4 %all-reduce.4.cloned.1.call-done = (f32[128,640]{1,0:T(8,128)}, f32[128,128]{1,0:T(8,128)}) async-done(((f32[128,640]{1,0:T(8,128)}, f32[128,128]{1,0:T(8,128)}), (f32[128,640]{1,0:T(8,128)}, f32[128,128]{1,0:T(8,128)})) %all-reduce.4.cloned.1.call-update) | async-done | bytes 393232 | tf_op jit(solution)/shard_map/psum | solution.py:95
  576.3 1.7 broadcast_multiply_fusion
  578.1 1.5 broadcast_multiply_fusion.1
  (41 shorter events, 1.9 us)
Async XLA Ops:
  7.2 2.1 copy-start
  7.2 2.1 copy-start.8
  7.2 121.2 %all-gather.2.cloned.1.call-start = ((), (), s32[]{:S(2)}) async-start(), calls=%async_computation.1 | async-start | bytes 17825792 | tf_op jit(solution)/shard_map/all_gather | solution.py:43
  10.9 4.2 copy-start.1
  15.1 1.9 copy-start.9
  15.1 1.9 copy-start.12
  15.2 328.4 %reduce-scatter.2.cloned.1.call-start = ((), (), s32[]{:S(2)}) async-start(), calls=%async_computation.2 | async-start | bytes 17825792 | tf_op jit(solution)/shard_map/reduce_scatter | solution.py:70
  158.8 1.6 copy-start.2
  158.8 1.6 copy-start.7
  200.2 376.2 %all-reduce.4.cloned.1.call-start = ((), (), s32[]{:S(2)}) async-start(), calls=%async_computation.3 | async-start | bytes 786432 | tf_op jit(solution)/shard_map/psum | solution.py:95
  214.0 3.8 copy-start.5
  214.0 3.8 copy-start.10
  343.6 3.6 copy-start.3
  347.2 4.2 copy-start.6
  347.2 4.2 copy-start.11
  365.1 3.3 copy-start.4
Sparse Core Ops, SparseCore 0:
  15.3 113.0 all-gather.1
  200.3 143.2 reduce-scatter.1
  435.5 140.7 all-reduce.3
where the time goes:
time: 588 us; the launch traced here: 586 us
  waiting for transfers between devices  365 us (62%)
  blocking collectives  64.4 us (11%)
  local copies, waits for them, and re-layouts  56.1 us (10%)
  matrix products  54.5 us (9%)
  other arithmetic  31.1 us (5%)
  between operations  13.9 us (2%)
    psum x1, waiting for transfers between devices, local(): lax.psum((local_in, local_out, local_gi, local_gx), ('dp', 'axial'))  140 us
    reduce_scatter x1, waiting for transfers between devices, local(): lax.psum_scatter(jnp.einsum('ijc,ikc->jkc', sub_grad, left, preferred_ele...  117 us
    all_gather x1, waiting for transfers between devices, local(): lax.all_gather(right, 'axial', axis=0, tiled=True)  108 us
    psum x1, blocking collectives, local(): lax.psum((local_in, local_out, local_gi, local_gx), ('dp', 'axial'))  64.4 us
    dot_general x1, local copies, waits for them, and re-layouts, local(): jnp.einsum('ijc,ikc->jkc', sub_grad, left, preferred_element_type=jnp.flo...  24.3 us
    all_gather x1, local copies, waits for them, and re-layouts, local(): lax.all_gather(right, 'axial', axis=0, tiled=True)  22.1 us
    unnamed x4, other arithmetic  16.3 us
    dot_general x1, matrix products, local(): jnp.einsum('ijc,ikc->jkc', sub_grad, left, preferred_element_type=jnp.flo...  12.2 us
  transfers between devices with their start and end apart: 3, of which 3 were waited for; matrix products, arithmetic and copies ran while one was open for 5% of the time, Pallas kernels for 0%

commit v1 on v0

v1 whole, which is shorter than its diff:
```python
import functools

import jax
import jax.numpy as jnp
from jax import lax
from jax.experimental import pallas as pl
from jax.experimental.pallas import tpu as pltpu
from jax.sharding import PartitionSpec as P

MESH = pl.DeviceIdType.MESH
F32 = jnp.float32
BF16 = jnp.bfloat16
LEFT, RIGHT, PROD, GPROD, GLEFT, GRIGHT = range(6)


def dot(a, b):
    return lax.dot_general(a, b, (((1,), (0,)), ((), ())), preferred_element_type=F32)


def dot_nt(a, b):
    return lax.dot_general(a, b, (((1,), (1,)), ((), ())), preferred_element_type=F32)


def dot_tn(a, b):
    return lax.dot_general(a, b, (((0,), (0,)), ((), ())), preferred_element_type=F32)


def sigmoid(v):
    return 0.5 * jnp.tanh(0.5 * v) + 0.5


def stats(v):
    center = jnp.mean(v, axis=0, keepdims=True)
    shifted = v - center
    inv = lax.rsqrt(jnp.mean(shifted * shifted, axis=0, keepdims=True) + 1e-05)
    return shifted * inv, inv


def kernel(
    n_dp, n_ax, factor,
    pair, cot, w_in, w_out, gain_in, gain_x,
    upd, gpair, gw_in, gw_out, ggi, ggx,
    send, recv, tbuf, tbuf2, lc, rc, gc,
    normed, unit_in, inv_in, gate_a, q_a, gate_b, q_b, gate_o, s_x, c_g, glift, xnorm, gnorm,
    w_t, wo_t, gin, gx, dw, r1, r2, s1, s2, fin,
    ssem, rsem, lsem, asend, arecv,
):
    me = lax.axis_index("axial")
    dp = lax.axis_index("dp")
    my_z, my_y, my_c = me // 4, (me // 2) % 2, me % 2

    def peer(o):
        return ((my_z + o // 4) % 4) * 4 + ((my_y + (o // 2) % 2) % 2) * 2 + (my_c + o % 2) % 2

    def dp_peer(o):
        return (dp + o) % n_dp

    def each(lo, hi, fn, unroll=1):
        def body(i, carry):
            fn(i)
            return carry
        lax.fori_loop(lo, hi, body, 0, unroll=unroll)

    barrier = pltpu.get_barrier_semaphore()
    each(1, n_ax, lambda o: pl.semaphore_signal(
        barrier, inc=1, device_id=(dp, peer(o)), device_id_type=MESH))
    each(1, n_dp, lambda o: pl.semaphore_signal(
        barrier, inc=1, device_id=(dp_peer(o), me), device_id_type=MESH))

    def start(t):
        def one(o):
            d = peer(o)
            pltpu.make_async_remote_copy(
                src_ref=send.at[t, d], dst_ref=recv.at[t, me],
                send_sem=ssem.at[t], recv_sem=rsem.at[t],
                device_id=(dp, d), device_id_type=MESH).start()
        each(1, n_ax, one)
        pltpu.make_async_copy(send.at[t, me], recv.at[t, me], lsem.at[t]).start()

    def wait_recv(t):
        pltpu.make_async_copy(send.at[t, me], recv.at[t, me], lsem.at[t]).wait()
        part = recv.at[t, pl.ds(0, n_ax - 1)]
        pltpu.make_async_copy(part, part, rsem.at[t]).wait()

    def wait_send(t):
        part = send.at[t, pl.ds(0, n_ax - 1)]
        pltpu.make_async_copy(part, part, ssem.at[t]).wait()

    def reduce_start(p):
        def one(o):
            d = peer(o)
            pltpu.make_async_remote_copy(
                src_ref=dw.at[p, pl.ds(8 * d, 8)], dst_ref=r1.at[p, me],
                send_sem=asend.at[p], recv_sem=arecv.at[p],
                device_id=(dp, d), device_id_type=MESH).start()
        each(1, n_ax, one)
        r1[p, me] = dw[p, pl.ds(8 * me, 8)]

    def reduce_dp(p):
        part = r1.at[p, pl.ds(0, n_ax - 1)]
        pltpu.make_async_copy(part, part, arecv.at[p]).wait()
        total = jnp.sum(r1[p], axis=0)
        s1[p] = total
        r2[p, dp] = total

        def one(o):
            pltpu.make_async_remote_copy(
                src_ref=s1.at[p], dst_ref=r2.at[p, dp],
                send_sem=asend.at[3 + p], recv_sem=arecv.at[3 + p],
                device_id=(dp_peer(o), me), device_id_type=MESH).start()
        each(1, n_dp, one)

    def reduce_back(p):
        part = r2.at[p, pl.ds(0, n_dp - 1)]
        pltpu.make_async_copy(part, part, arecv.at[3 + p]).wait()
        total = jnp.sum(r2[p], axis=0) * factor
        s2[p] = total
        fin[p, me] = total

        def one(o):
            pltpu.make_async_remote_copy(
                src_ref=s2.at[p], dst_ref=fin.at[p, me],
                send_sem=asend.at[6 + p], recv_sem=arecv.at[6 + p],
                device_id=(dp, peer(o)), device_id_type=MESH).start()
        each(1, n_ax, one)

    def reduce_end(p):
        part = fin.at[p, pl.ds(0, n_ax - 1)]
        pltpu.make_async_copy(part, part, arecv.at[6 + p]).wait()

    def reduce_sent(p):
        part = r1.at[p, pl.ds(0, n_ax - 1)]
        pltpu.make_async_copy(part, part, asend.at[p]).wait()
        part = r2.at[p, pl.ds(0, n_dp - 1)]
        pltpu.make_async_copy(part, part, asend.at[3 + p]).wait()
        part = fin.at[p, pl.ds(0, n_ax - 1)]
        pltpu.make_async_copy(part, part, asend.at[6 + p]).wait()

    def strided(i):
        return pl.ds(i, 128, stride=8)

    def put(k, values):
        tbuf2[0, strided(k), :] = values[:, :128]
        tbuf2[1, strided(k), :] = values[:, 128:]

    def take(k):
        return jnp.concatenate([tbuf[0, strided(k), :], tbuf[1, strided(k), :]], axis=1)

    def flush(t):
        for n in range(2):
            send[t, :, :, 128 * n:128 * (n + 1)] = tbuf2[n].astype(BF16).reshape(16, 64, 128)

    def unpack(t):
        for n in range(2):
            tbuf[n] = recv[t, :, :, 128 * n:128 * (n + 1)].astype(F32).reshape(1024, 128)

    def load_pair(t, cp):
        both = recv[t, :, pl.ds(pl.multiple_of(16 * cp, 16), 16), :].astype(F32).reshape(16, 2, 8, 256)
        return both[:, 0], both[:, 1]

    def store_pair(t, cp, even, odd):
        both = jnp.concatenate([even, odd], axis=1).astype(BF16)
        send[t, :, pl.ds(pl.multiple_of(16 * cp, 16), 16), :] = both

    w_t[...] = w_in[...].astype(F32).T.astype(BF16)
    wo_t[...] = w_out[...].astype(F32).T.astype(BF16)
    gin[...] = jnp.broadcast_to(jnp.broadcast_to(gain_in[...], (128, 128)).T[:, :1], (128, 256))
    gx[...] = jnp.broadcast_to(jnp.broadcast_to(gain_x[...], (128, 128)).T[:, :1], (128, 256))

    for h in range(2):
        def left_row(k):
            i = 8 * h + k
            unit, inv = stats(pair[i].astype(F32).T)
            unit_in[i] = unit
            inv_in[i] = inv
            flat = (unit * gin[...]).astype(BF16)
            normed[i] = flat
            projected = dot(w_t[0:256], flat)
            value, gate = projected[:128], sigmoid(projected[128:])
            left = value * gate
            gate_a[i] = gate
            q_a[i] = left * (1.0 - gate)
            put(k, left)
        each(0, 8, left_row)
        flush(2 * LEFT + h)
        if h == 0:
            pl.semaphore_wait(barrier, n_ax - 1 + n_dp - 1)
        start(2 * LEFT + h)

    for h in range(2):
        def right_row(k):
            i = 8 * h + k
            projected = dot(w_t[256:512], normed[i])
            value, gate = projected[:128], sigmoid(projected[128:])
            right = value * gate
            gate_b[i] = gate
            q_b[i] = right * (1.0 - gate)
            put(k, right)
        each(0, 8, right_row)
        flush(2 * RIGHT + h)
        start(2 * RIGHT + h)

    def gate_row(i):
        gate = sigmoid(dot(w_t[512:640], normed[i]))
        upstream = cot[i].astype(F32).T
        lift = upstream * gate
        gate_o[i] = gate
        c_g[i] = lift * (1.0 - gate)
        lift = lift.astype(BF16)
        glift[i] = lift
        s_x[i] = dot(w_out[...], lift) * gx[...]
    each(0, 16, gate_row)

    for t in (2 * LEFT, 2 * LEFT + 1, 2 * RIGHT, 2 * RIGHT + 1):
        wait_recv(t)

    def product_pair(cp):
        left0, left1 = load_pair(2 * LEFT, cp), load_pair(2 * LEFT + 1, cp)
        right0, right1 = load_pair(2 * RIGHT, cp), load_pair(2 * RIGHT + 1, cp)
        prods = []
        for e in range(2):
            left = jnp.concatenate([left0[e], left1[e]], axis=0).reshape(256, 256).astype(BF16)
            right = jnp.concatenate([right0[e], right1[e]], axis=1).reshape(256, 256).astype(BF16)
            lc[2 * cp + e] = left
            rc[2 * cp + e] = right
            prods.append(dot_nt(left, right).reshape(2, 16, 8, 256))
        for h in range(2):
            store_pair(2 * PROD + h, cp, prods[0][h], prods[1][h])
    each(0, 4, product_pair)
    start(2 * PROD)
    start(2 * PROD + 1)

    for h in range(2):
        wait_recv(2 * PROD + h)
        unpack(2 * PROD + h)

        def norm_row(k):
            i = 8 * h + k
            unit, inv = stats(take(k))
            xnorm[i] = (unit * gx[...]).astype(BF16)
            scaled = s_x[i]
            mean_one = jnp.mean(scaled, axis=0, keepdims=True)
            mean_two = jnp.mean(scaled * unit, axis=0, keepdims=True)
            put(k, (scaled - mean_one - unit * mean_two) * inv)
        each(0, 8, norm_row)
        flush(2 * GPROD + h)
        start(2 * GPROD + h)

    dw[...] = jnp.zeros_like(dw)

    def lift_row(i):
        flat = xnorm[i]
        lifted = dot(wo_t[...], flat)
        upd[i] = (gate_o[i] * lifted).T.astype(BF16)
        ggate = (lifted * c_g[i]).astype(BF16)
        dw[0, :, 0:128] += dot_nt(flat, glift[i])
        dw[0, :, 128:256] += dot_nt(normed[i], ggate)
        gnorm[i] = dot(w_in[:, 512:640], ggate)
    each(0, 16, lift_row)
    reduce_start(0)

    for h in range(2):
        wait_recv(2 * GPROD + h)

        def gleft_pair(cp):
            grads = load_pair(2 * GPROD + h, cp)
            outs = []
            for e in range(2):
                grad = grads[e].reshape(128, 256).astype(BF16)
                gc[2 * cp + e, pl.ds(128 * h, 128), :] = grad
                outs.append(dot(grad, rc[2 * cp + e]).reshape(16, 8, 256))
            store_pair(2 * GLEFT + h, cp, outs[0], outs[1])
        each(0, 4, gleft_pair)
        start(2 * GLEFT + h)

    def gright_pair(cp):
        outs = [dot_tn(gc[2 * cp + e], lc[2 * cp + e]).reshape(16, 2, 8, 256) for e in range(2)]
        for h in range(2):
            store_pair(2 * GRIGHT + h, cp, outs[0][:, h], outs[1][:, h])
    each(0, 4, gright_pair)
    start(2 * GRIGHT)
    start(2 * GRIGHT + 1)
    reduce_dp(0)

    def back(a, p, lo, gate_ref, q_ref):
        for h in range(2):
            wait_recv(2 * a + h)
            unpack(2 * a + h)

            def back_row(k):
                i = 8 * h + k
                grad = take(k)
                both = jnp.concatenate([grad * gate_ref[i], grad * q_ref[i]], axis=0).astype(BF16)
                dw[p] += dot_nt(normed[i], both)
                gnorm[i] += dot(w_in[:, lo:lo + 256], both)
            each(0, 8, back_row)

    back(GLEFT, 1, 0, gate_a, q_a)
    reduce_start(1)
    reduce_back(0)
    reduce_dp(1)
    back(GRIGHT, 2, 256, gate_b, q_b)
    reduce_start(2)
    reduce_back(1)

    def out_row(i):
        unit = unit_in[i]
        scaled = gnorm[i] * gin[...]
        mean_one = jnp.mean(scaled, axis=0, keepdims=True)
        mean_two = jnp.mean(scaled * unit, axis=0, keepdims=True)
        gpair[i] = ((scaled - mean_one - unit * mean_two) * inv_in[i]).T.astype(BF16)
    each(0, 8, out_row)
    reduce_dp(2)
    each(8, 16, out_row)
    reduce_back(2)
    reduce_end(0)
    reduce_end(1)
    reduce_end(2)

    first = fin[0].reshape(128, 256)
    gw_out[...] = first[:, :128]
    gw_in[:, 512:640] = first[:, 128:]
    gw_in[:, 0:256] = fin[1].reshape(128, 256)
    gw_in[:, 256:512] = fin[2].reshape(128, 256)
    row_in = jnp.sum(gw_in[...] * w_in[...].astype(F32), axis=1, keepdims=True)
    row_x = jnp.sum(gw_out[...] * w_out[...].astype(F32), axis=1, keepdims=True)
    ggi[...] = jnp.broadcast_to(row_in, (128, 128)).T[:1] / gain_in[...]
    ggx[...] = jnp.broadcast_to(row_x, (128, 128)).T[:1] / gain_x[...]

    for t in range(12):
        wait_send(t)
    for p in range(3):
        reduce_sent(p)


def local(n_dp, n_ax, pair, cotangent, in_weight, out_weight, gain_in, gain_x):
    rows, width, chan = pair.shape[1:]
    factor = 1.0 / (n_dp * width * width) ** 0.5
    vmem = pl.BlockSpec(memory_space=pltpu.VMEM)
    cells = (rows, chan, width)
    outs = pl.pallas_call(
        functools.partial(kernel, n_dp, n_ax, factor),
        name="triangle",
        out_shape=(
            jax.ShapeDtypeStruct((rows, width, chan), BF16),
            jax.ShapeDtypeStruct((rows, width, chan), BF16),
            jax.ShapeDtypeStruct((128, 640), F32),
            jax.ShapeDtypeStruct((128, 128), F32),
            jax.ShapeDtypeStruct((1, 128), F32),
            jax.ShapeDtypeStruct((1, 128), F32),
        ),
        in_specs=[vmem] * 6,
        out_specs=(vmem,) * 6,
        scratch_shapes=[
            pltpu.VMEM((12, 16, 64, 256), BF16),
            pltpu.VMEM((12, 16, 64, 256), BF16),
            pltpu.VMEM((2, 1024, 128), F32),
            pltpu.VMEM((2, 1024, 128), F32),
            pltpu.VMEM((8, 256, 256), BF16),
            pltpu.VMEM((8, 256, 256), BF16),
            pltpu.VMEM((8, 256, 256), BF16),
            pltpu.VMEM(cells, BF16),
            pltpu.VMEM(cells, F32),
            pltpu.VMEM((rows, 1, width), F32),
            pltpu.VMEM(cells, F32),
            pltpu.VMEM(cells, F32),
            pltpu.VMEM(cells, F32),
            pltpu.VMEM(cells, F32),
            pltpu.VMEM(cells, F32),
            pltpu.VMEM(cells, F32),
            pltpu.VMEM(cells, F32),
            pltpu.VMEM(cells, BF16),
            pltpu.VMEM(cells, BF16),
            pltpu.VMEM(cells, F32),
            pltpu.VMEM((640, 128), BF16),
            pltpu.VMEM((128, 128), BF16),
            pltpu.VMEM((128, 256), F32),
            pltpu.VMEM((128, 256), F32),
            pltpu.VMEM((3, 128, 256), F32),
            pltpu.VMEM((3, 16, 8, 256), F32),
            pltpu.VMEM((3, 8, 8, 256), F32),
            pltpu.VMEM((3, 8, 256), F32),
            pltpu.VMEM((3, 8, 256), F32),
            pltpu.VMEM((3, 16, 8, 256), F32),
            pltpu.SemaphoreType.DMA((12,)),
            pltpu.SemaphoreType.DMA((12,)),
            pltpu.SemaphoreType.DMA((12,)),
            pltpu.SemaphoreType.DMA((9,)),
            pltpu.SemaphoreType.DMA((9,)),
        ],
        compiler_params=pltpu.CompilerParams(
            collective_id=0, has_side_effects=True, vmem_limit_bytes=60 * 2**20),
        cost_estimate=pl.CostEstimate(
            flops=3_300_000_000, bytes_accessed=5_000_000, transcendentals=1_600_000),
    )(pair[0], cotangent[0], in_weight, out_weight, gain_in[None], gain_x[None])
    upd, gpair, gw_in, gw_out, ggi, ggx = outs
    return upd[None], gpair[None], gw_in, gw_out, ggi[0], ggx[0]


def solution(mesh):
    cells = P("dp", "axial", None, None)
    n_dp, n_ax = mesh.shape["dp"], mesh.shape["axial"]
    return jax.shard_map(
        functools.partial(local, n_dp, n_ax), mesh=mesh,
        in_specs=(cells, cells, P(), P(), P(), P()),
        out_specs=(cells, cells, P(), P(), P(), P()), check_vma=False)
```

time: 588 us -> 118 us (0.20)
  waiting for transfers between devices: 365 us -> 0 us
  Pallas kernels: 0 us -> 111 us
  blocking collectives: 64.4 us -> 0 us
  matrix products: 54.5 us -> 0 us
  local copies, waits for them, and re-layouts: 56.1 us -> 6.23 us
  other arithmetic: 31.1 us -> 0 us
  between operations: 13.9 us -> 0.66 us
    psum x1 -> x0, waiting for transfers between devices: 140 us -> none  [local(): lax.psum((local_in, local_out, local_gi, local_gx), ('dp', 'axial'))]
    reduce_scatter x1 -> x0, waiting for transfers between devices: 117 us -> none  [local(): lax.psum_scatter(jnp.einsum('ijc,ikc->jkc', sub_grad, left, preferred_ele...]
    pallas_call x0 -> x1, Pallas kernels: none -> 111 us  [local(): pl.pallas_call(functools.partial(kernel, n_dp, n_ax, factor), name='trian...]
    all_gather x1 -> x0, waiting for transfers between devices: 108 us -> none  [local(): lax.all_gather(right, 'axial', axis=0, tiled=True)]
    psum x1 -> x0, blocking collectives: 64.4 us -> none  [local(): lax.psum((local_in, local_out, local_gi, local_gx), ('dp', 'axial'))]
    dot_general x9 -> x0, matrix products: 54.5 us -> none  [the longest x1 12.2 us: local(): jnp.einsum('ijc,ikc->jkc', sub_grad, left, preferred_element_type=jnp.flo...]
    dot_general x2 -> x0, local copies, waits for them, and re-layouts: 26.7 us -> none  [the longest x1 24.3 us: local(): jnp.einsum('ijc,ikc->jkc', sub_grad, left, preferred_element_type=jnp.flo...]
    all_gather x1 -> x0, local copies, waits for them, and re-layouts: 22.1 us -> none  [local(): lax.all_gather(right, 'axial', axis=0, tiled=True)]
  transfers between devices with their start and end apart: 3 -> 0, of which waited for: 3 -> 0; matrix products, arithmetic and copies ran while one was open for 5% -> 0% of each run, Pallas kernels for 0% -> 0%
where the time goes in v1:
time: 118 us
  Pallas kernels  111 us (94%)
  local copies, waits for them, and re-layouts  6.23 us (5%)
    pallas_call x1, Pallas kernels, local(): pl.pallas_call(functools.partial(kernel, n_dp, n_ax, factor), name='trian...  111 us
    unnamed x16, local copies, waits for them, and re-layouts  6.23 us

profile of v1, /device:TPU:1, one launch (start us, length us, event | category | flops | bytes accessed | tf_op | source)
XLA Modules:
  0.0 118.2 jit_solution(17402351210261792176)
XLA Ops:
  0.6 111.3 %triangle.1 = (bf16[16,256,128]{2,1,0:T(8,128)(2,1)}, bf16[16,256,128]{2,1,0:T(8,128)(2,1)}, f32[128,640]{1,0:T(8,128)}, f32[128,128]{1,0:T(8,128)}, f32[1,128]{1,0:T(1,128)}, /*index=5*/f32[1,128]{1,0:T(1,128)}) custom-call(bf16[16,256,128]{2,1,0:T(8,128)(2,1)} %bitcast.10, bf16[16,256,128]{2,1,0:T(8,128)(2,1)} %bitcast.11, bf16[128,640]{1,0:T(8,128)(2,1)} %w_in.1, ...), custom_call_target="tpu_custom_call" | custom-call | flops 3300000000 | bytes 5000000 | tf_op jit(solution)/shard_map/triangle/pallas_call | solution.py:341
  112.0 0.0 copy-start
  112.0 2.4 %copy.18 = bf16[1,16,256,128]{3,2,1,0:T(8,128)(2,1)} copy(bf16[1,16,256,128]{3,2,1,0:T(8,128)(2,1)} %bitcast.9) | data formatting | bytes 2097152
  114.4 0.0 copy-done
  114.4 0.0 copy-start.1
  114.4 1.0 copy.19
  115.3 0.2 copy-done.1
  115.5 0.0 copy-start.2
  115.5 0.7 copy.20
  116.3 0.1 copy-done.2
  116.4 0.0 copy-start.4
  116.4 0.6 copy.21
  117.0 0.0 copy-done.4
  117.0 0.0 copy-start.3
  117.0 0.5 copy.22
  117.5 0.2 copy-done.3
  117.7 0.5 copy.23
Async XLA Ops:
  112.0 2.4 %copy-start = (bf16[16,256,128]{2,1,0:T(8,128)(2,1)S(1)}, bf16[16,256,128]{2,1,0:T(8,128)(2,1)}, u32[]{:S(2)}) copy-start(bf16[16,256,128]{2,1,0:T(8,128)(2,1)} %get-tuple-element.13) | copy-start | bytes 3145732
  114.4 1.2 copy-start.1
  115.5 0.9 copy-start.2
  116.4 0.6 copy-start.4
  117.0 0.7 copy-start.3

commit v2 on v1

--- a/solution.py
+++ b/solution.py
@@ -38,8 +38,10 @@
 
 def kernel(
     n_dp, n_ax, factor,
+    pair_h, cot_h, w_in_h, w_out_h, gain_in_h, gain_x_h,
+    upd_h, gpair_h, gw_in_h, gw_out_h, ggi_h, ggx_h,
     pair, cot, w_in, w_out, gain_in, gain_x,
-    upd, gpair, gw_in, gw_out, ggi, ggx,
+    upd, gpair, gw_in, gw_out, ggi, ggx, isem, osem, gproj,
     send, recv, tbuf, tbuf2, lc, rc, gc,
     normed, unit_in, inv_in, gate_a, q_a, gate_b, q_b, gate_o, s_x, c_g, glift, xnorm, gnorm,
     w_t, wo_t, gin, gx, dw, r1, r2, s1, s2, fin,
@@ -66,6 +68,34 @@
         barrier, inc=1, device_id=(dp, peer(o)), device_id_type=MESH))
     each(1, n_dp, lambda o: pl.semaphore_signal(
         barrier, inc=1, device_id=(dp_peer(o), me), device_id_type=MESH))
+
+    half = pl.ds(0, 8), pl.ds(8, 8)
+    in_pairs = {
+        "w_in": (w_in_h, w_in), "gain_in": (gain_in_h, gain_in),
+        "pair0": (pair_h.at[half[0]], pair.at[half[0]]), "pair1": (pair_h.at[half[1]], pair.at[half[1]]),
+        "w_out": (w_out_h, w_out), "gain_x": (gain_x_h, gain_x), "cot": (cot_h, cot),
+    }
+    out_pairs = {
+        "upd": (upd, upd_h),
+        "gpair0": (gpair.at[half[0]], gpair_h.at[half[0]]), "gpair1": (gpair.at[half[1]], gpair_h.at[half[1]]),
+        "gw_in": (gw_in, gw_in_h), "gw_out": (gw_out, gw_out_h), "ggi": (ggi, ggi_h), "ggx": (ggx, ggx_h),
+    }
+    in_names, put_names = list(in_pairs), list(out_pairs)
+
+    def in_copy(name):
+        return pltpu.make_async_copy(*in_pairs[name], isem.at[in_names.index(name)])
+
+    def out_copy(name):
+        return pltpu.make_async_copy(*out_pairs[name], osem.at[put_names.index(name)])
+
+    def fetch(name):
+        in_copy(name).wait()
+
+    def put_out(name):
+        out_copy(name).start()
+
+    for name in in_names:
+        in_copy(name).start()
 
     def start(t):
         def one(o):
@@ -162,43 +192,60 @@
         both = jnp.concatenate([even, odd], axis=1).astype(BF16)
         send[t, :, pl.ds(pl.multiple_of(16 * cp, 16), 16), :] = both
 
+    fetch("w_in")
     w_t[...] = w_in[...].astype(F32).T.astype(BF16)
+    fetch("gain_in")
+    gin[...] = jnp.broadcast_to(jnp.broadcast_to(gain_in[...], (128, 128)).T[:, :1], (128, 256))
+
+    def norm_in(i):
+        unit, inv = stats(pair[i].astype(F32).T)
+        unit_in[i] = unit
+        inv_in[i] = inv
+        normed[i] = (unit * gin[...]).astype(BF16)
+
+    def gated(i, k, lo, gate_ref, q_ref):
+        projected = dot(w_t[lo:lo + 256], normed[i])
+        gate = sigmoid(projected[128:])
+        value = projected[:128] * gate
+        gate_ref[i] = gate
+        q_ref[i] = value * (1.0 - gate)
+        put(k, value)
+
+    def first_left(k):
+        norm_in(k)
+        gated(k, k, 0, gate_a, q_a)
+
+    def first_right(k):
+        gated(k, k, 256, gate_b, q_b)
+
+    def second_right(k):
+        norm_in(8 + k)
+        gated(8 + k, k, 256, gate_b, q_b)
+
+    def second_left(k):
+        gated(8 + k, k, 0, gate_a, q_a)
+
+    fetch("pair0")
+    each(0, 8, first_left)
+    flush(2 * LEFT)
+    pl.semaphore_wait(barrier, n_ax - 1 + n_dp - 1)
+    start(2 * LEFT)
+    each(0, 8, first_right)
+    flush(2 * RIGHT)
+    start(2 * RIGHT)
+    fetch("pair1")
+    each(0, 8, second_right)
+    flush(2 * RIGHT + 1)
+    start(2 * RIGHT + 1)
+    each(0, 8, second_left)
+    flush(2 * LEFT + 1)
+    start(2 * LEFT + 1)
+
+    fetch("w_out")
+    fetch("gain_x")
+    fetch("cot")
     wo_t[...] = w_out[...].astype(F32).T.astype(BF16)
-    gin[...] = jnp.broadcast_to(jnp.broadcast_to(gain_in[...], (128, 128)).T[:, :1], (128, 256))
     gx[...] = jnp.broadcast_to(jnp.broadcast_to(gain_x[...], (128, 128)).T[:, :1], (128, 256))
-
-    for h in range(2):
-        def left_row(k):
-            i = 8 * h + k
-            unit, inv = stats(pair[i].astype(F32).T)
-            unit_in[i] = unit
-            inv_in[i] = inv
-            flat = (unit * gin[...]).astype(BF16)
-            normed[i] = flat
-            projected = dot(w_t[0:256], flat)
-            value, gate = projected[:128], sigmoid(projected[128:])
-            left = value * gate
-            gate_a[i] = gate
-            q_a[i] = left * (1.0 - gate)
-            put(k, left)
-        each(0, 8, left_row)
-        flush(2 * LEFT + h)
-        if h == 0:
-            pl.semaphore_wait(barrier, n_ax - 1 + n_dp - 1)
-        start(2 * LEFT + h)
-
-    for h in range(2):
-        def right_row(k):
-            i = 8 * h + k
-            projected = dot(w_t[256:512], normed[i])
-            value, gate = projected[:128], sigmoid(projected[128:])
-            right = value * gate
-            gate_b[i] = gate
-            q_b[i] = right * (1.0 - gate)
-            put(k, right)
-        each(0, 8, right_row)
-        flush(2 * RIGHT + h)
-        start(2 * RIGHT + h)
 
     def gate_row(i):
         gate = sigmoid(dot(w_t[512:640], normed[i]))
@@ -210,25 +257,32 @@
         glift[i] = lift
         s_x[i] = dot(w_out[...], lift) * gx[...]
     each(0, 16, gate_row)
-
-    for t in (2 * LEFT, 2 * LEFT + 1, 2 * RIGHT, 2 * RIGHT + 1):
-        wait_recv(t)
-
-    def product_pair(cp):
-        left0, left1 = load_pair(2 * LEFT, cp), load_pair(2 * LEFT + 1, cp)
-        right0, right1 = load_pair(2 * RIGHT, cp), load_pair(2 * RIGHT + 1, cp)
-        prods = []
-        for e in range(2):
-            left = jnp.concatenate([left0[e], left1[e]], axis=0).reshape(256, 256).astype(BF16)
-            right = jnp.concatenate([right0[e], right1[e]], axis=1).reshape(256, 256).astype(BF16)
-            lc[2 * cp + e] = left
-            rc[2 * cp + e] = right
-            prods.append(dot_nt(left, right).reshape(2, 16, 8, 256))
-        for h in range(2):
-            store_pair(2 * PROD + h, cp, prods[0][h], prods[1][h])
-    each(0, 4, product_pair)
-    start(2 * PROD)
-    start(2 * PROD + 1)
+    dw[...] = jnp.zeros_like(dw)
+
+    wait_recv(2 * LEFT)
+    wait_recv(2 * RIGHT)
+    wait_recv(2 * RIGHT + 1)
+    for h in range(2):
+        if h == 1:
+            wait_recv(2 * LEFT + 1)
+
+        def product_pair(cp):
+            lefts = load_pair(2 * LEFT + h, cp)
+            if h == 0:
+                right0, right1 = load_pair(2 * RIGHT, cp), load_pair(2 * RIGHT + 1, cp)
+            prods = []
+            for e in range(2):
+                left = lefts[e].reshape(128, 256).astype(BF16)
+                lc[2 * cp + e, 128 * h:128 * (h + 1)] = left
+                if h == 0:
+                    right = jnp.concatenate([right0[e], right1[e]], axis=1).reshape(256, 256).astype(BF16)
+                    rc[2 * cp + e] = right
+                else:
+                    right = rc[2 * cp + e]
+                prods.append(dot_nt(left, right).reshape(16, 8, 256))
+            store_pair(2 * PROD + h, cp, prods[0], prods[1])
+        each(0, 4, product_pair)
+        start(2 * PROD + h)
 
     for h in range(2):
         wait_recv(2 * PROD + h)
@@ -246,8 +300,6 @@
         flush(2 * GPROD + h)
         start(2 * GPROD + h)
 
-    dw[...] = jnp.zeros_like(dw)
-
     def lift_row(i):
         flat = xnorm[i]
         lifted = dot(wo_t[...], flat)
@@ -256,8 +308,6 @@
         dw[0, :, 0:128] += dot_nt(flat, glift[i])
         dw[0, :, 128:256] += dot_nt(normed[i], ggate)
         gnorm[i] = dot(w_in[:, 512:640], ggate)
-    each(0, 16, lift_row)
-    reduce_start(0)
 
     for h in range(2):
         wait_recv(2 * GPROD + h)
@@ -267,11 +317,14 @@
             outs = []
             for e in range(2):
                 grad = grads[e].reshape(128, 256).astype(BF16)
-                gc[2 * cp + e, pl.ds(128 * h, 128), :] = grad
+                gc[2 * cp + e, 128 * h:128 * (h + 1)] = grad
                 outs.append(dot(grad, rc[2 * cp + e]).reshape(16, 8, 256))
             store_pair(2 * GLEFT + h, cp, outs[0], outs[1])
         each(0, 4, gleft_pair)
         start(2 * GLEFT + h)
+        each(8 * h, 8 * h + 8, lift_row)
+
+    reduce_start(0)
 
     def gright_pair(cp):
         outs = [dot_tn(gc[2 * cp + e], lc[2 * cp + e]).reshape(16, 2, 8, 256) for e in range(2)]
@@ -280,78 +333,115 @@
     each(0, 4, gright_pair)
     start(2 * GRIGHT)
     start(2 * GRIGHT + 1)
+    put_out("upd")
+
+    def back_row(k, h, p, gate_ref, q_ref):
+        i = 8 * h + k
+        grad = take(k)
+        both = jnp.concatenate([grad * gate_ref[i], grad * q_ref[i]], axis=0).astype(BF16)
+        gproj[k] = both
+        dw[p] += dot_nt(normed[i], both)
+
+    def back_a(h):
+        def grad_row(k):
+            back_row(k, h, 1, gate_a, q_a)
+            gnorm[8 * h + k] += dot(w_in[:, 0:256], gproj[k])
+        wait_recv(2 * GLEFT + h)
+        unpack(2 * GLEFT + h)
+        each(0, 8, grad_row)
+
+    def back_b(h):
+        def grad_row(k):
+            back_row(k, h, 2, gate_b, q_b)
+        wait_recv(2 * GRIGHT + h)
+        unpack(2 * GRIGHT + h)
+        each(0, 8, grad_row)
+
+    def out_rows(h):
+        def out_row(k):
+            i = 8 * h + k
+            unit = unit_in[i]
+            scaled = (gnorm[i] + dot(w_in[:, 256:512], gproj[k])) * gin[...]
+            mean_one = jnp.mean(scaled, axis=0, keepdims=True)
+            mean_two = jnp.mean(scaled * unit, axis=0, keepdims=True)
+            gpair[i] = ((scaled - mean_one - unit * mean_two) * inv_in[i]).T.astype(BF16)
+        each(0, 8, out_row)
+        put_out("gpair%d" % h)
+
+    back_a(0)
+    back_a(1)
+    reduce_start(1)
+    back_b(0)
     reduce_dp(0)
-
-    def back(a, p, lo, gate_ref, q_ref):
-        for h in range(2):
-            wait_recv(2 * a + h)
-            unpack(2 * a + h)
-
-            def back_row(k):
-                i = 8 * h + k
-                grad = take(k)
-                both = jnp.concatenate([grad * gate_ref[i], grad * q_ref[i]], axis=0).astype(BF16)
-                dw[p] += dot_nt(normed[i], both)
-                gnorm[i] += dot(w_in[:, lo:lo + 256], both)
-            each(0, 8, back_row)
-
-    back(GLEFT, 1, 0, gate_a, q_a)
-    reduce_start(1)
+    out_rows(0)
+    back_b(1)
+    reduce_start(2)
+    reduce_dp(1)
+    out_rows(1)
+    reduce_dp(2)
     reduce_back(0)
-    reduce_dp(1)
-    back(GRIGHT, 2, 256, gate_b, q_b)
-    reduce_start(2)
     reduce_back(1)
-
-    def out_row(i):
-        unit = unit_in[i]
-        scaled = gnorm[i] * gin[...]
-        mean_one = jnp.mean(scaled, axis=0, keepdims=True)
-        mean_two = jnp.mean(scaled * unit, axis=0, keepdims=True)
-        gpair[i] = ((scaled - mean_one - unit * mean_two) * inv_in[i]).T.astype(BF16)
-    each(0, 8, out_row)
-    reduce_dp(2)
-    each(8, 16, out_row)
-    reduce_back(2)
     reduce_end(0)
     reduce_end(1)
-    reduce_end(2)
-
     first = fin[0].reshape(128, 256)
     gw_out[...] = first[:, :128]
     gw_in[:, 512:640] = first[:, 128:]
     gw_in[:, 0:256] = fin[1].reshape(128, 256)
-    gw_in[:, 256:512] = fin[2].reshape(128, 256)
-    row_in = jnp.sum(gw_in[...] * w_in[...].astype(F32), axis=1, keepdims=True)
-    row_x = jnp.sum(gw_out[...] * w_out[...].astype(F32), axis=1, keepdims=True)
-    ggi[...] = jnp.broadcast_to(row_in, (128, 128)).T[:1] / gain_in[...]
+    row_x = jnp.sum(first[:, :128] * w_out[...].astype(F32), axis=1, keepdims=True)
     ggx[...] = jnp.broadcast_to(row_x, (128, 128)).T[:1] / gain_x[...]
-
+    reduce_back(2)
     for t in range(12):
         wait_send(t)
     for p in range(3):
         reduce_sent(p)
+    reduce_end(2)
+    gw_in[:, 256:512] = fin[2].reshape(128, 256)
+    row_in = jnp.sum(gw_in[...] * w_in[...].astype(F32), axis=1, keepdims=True)
+    ggi[...] = jnp.broadcast_to(row_in, (128, 128)).T[:1] / gain_in[...]
+    for name in ("gw_in", "gw_out", "ggi", "ggx"):
+        put_out(name)
+    for name in put_names:
+        out_copy(name).wait()
+
+
+def hand_on(*refs):
+    n = 6
+    sources, targets, held, sems = refs[:n], refs[n:2 * n], refs[2 * n:3 * n], refs[3 * n]
+    ins = [pltpu.make_async_copy(sources[k], held[k], sems.at[k]) for k in range(n)]
+    outs = [pltpu.make_async_copy(held[k], targets[k], sems.at[n + k]) for k in range(n)]
+    for copy in ins:
+        copy.start()
+    for k in range(n):
+        ins[k].wait()
+        outs[k].start()
+    for copy in outs:
+        copy.wait()
 
 
 def local(n_dp, n_ax, pair, cotangent, in_weight, out_weight, gain_in, gain_x):
     rows, width, chan = pair.shape[1:]
     factor = 1.0 / (n_dp * width * width) ** 0.5
-    vmem = pl.BlockSpec(memory_space=pltpu.VMEM)
+    anywhere = pl.BlockSpec(memory_space=pl.ANY)
     cells = (rows, chan, width)
+    args = (pair[0], cotangent[0], in_weight, out_weight, gain_in[None], gain_x[None])
+    out_shape = (
+        jax.ShapeDtypeStruct((rows, width, chan), BF16),
+        jax.ShapeDtypeStruct((rows, width, chan), BF16),
+        jax.ShapeDtypeStruct((128, 640), F32),
+        jax.ShapeDtypeStruct((128, 128), F32),
+        jax.ShapeDtypeStruct((1, 128), F32),
+        jax.ShapeDtypeStruct((1, 128), F32),
+    )
     outs = pl.pallas_call(
         functools.partial(kernel, n_dp, n_ax, factor),
         name="triangle",
-        out_shape=(
-            jax.ShapeDtypeStruct((rows, width, chan), BF16),
-            jax.ShapeDtypeStruct((rows, width, chan), BF16),
-            jax.ShapeDtypeStruct((128, 640), F32),
-            jax.ShapeDtypeStruct((128, 128), F32),
-            jax.ShapeDtypeStruct((1, 128), F32),
-            jax.ShapeDtypeStruct((1, 128), F32),
-        ),
-        in_specs=[vmem] * 6,
-        out_specs=(vmem,) * 6,
-        scratch_shapes=[
+        out_shape=out_shape,
+        in_specs=[pl.BlockSpec(memory_space=pltpu.HBM)] * 6,
+        out_specs=(anywhere,) * 6,
+        scratch_shapes=[pltpu.VMEM(v.shape, v.dtype) for v in args + out_shape] + [
+            pltpu.SemaphoreType.DMA((7,)),
+            pltpu.SemaphoreType.DMA((7,)),
+            pltpu.VMEM((8, 256, 256), BF16),
             pltpu.VMEM((12, 16, 64, 256), BF16),
             pltpu.VMEM((12, 16, 64, 256), BF16),
             pltpu.VMEM((2, 1024, 128), F32),
@@ -392,8 +482,17 @@
             collective_id=0, has_side_effects=True, vmem_limit_bytes=60 * 2**20),
         cost_estimate=pl.CostEstimate(
             flops=3_300_000_000, bytes_accessed=5_000_000, transcendentals=1_600_000),
-    )(pair[0], cotangent[0], in_weight, out_weight, gain_in[None], gain_x[None])
-    upd, gpair, gw_in, gw_out, ggi, ggx = outs
+    )(*args)
+    upd, gpair, gw_in, gw_out, ggi, ggx = pl.pallas_call(
+        hand_on,
+        name="hand_on",
+        out_shape=out_shape,
+        in_specs=[anywhere] * 6,
+        out_specs=(anywhere,) * 6,
+        scratch_shapes=[pltpu.VMEM(v.shape, v.dtype) for v in out_shape] + [
+            pltpu.SemaphoreType.DMA((12,))],
+        compiler_params=pltpu.CompilerParams(vmem_limit_bytes=60 * 2**20),
+    )(*outs)
     return upd[None], gpair[None], gw_in, gw_out, ggi[0], ggx[0]
 
 

time: 118 us -> 107 us (0.907)
  local copies, waits for them, and re-layouts: 6.23 us -> 0 us
  Pallas kernels: 111 us -> 106 us
    pallas_call x1, Pallas kernels: 111 us -> 103 us  [local(): pl.pallas_call(functools.partial(kernel, n_dp, n_ax, factor), name='trian...]
    unnamed x16 -> x0, local copies, waits for them, and re-layouts: 6.23 us -> none
    pallas_call x0 -> x1, Pallas kernels: none -> 2.76 us  [local(): pl.pallas_call(hand_on, name='hand_on', out_shape=out_shape, in_specs=[an...]
where the time goes in v2:
time: 107 us
  Pallas kernels  106 us (99%)
    pallas_call x1, Pallas kernels, local(): pl.pallas_call(functools.partial(kernel, n_dp, n_ax, factor), name='trian...  103 us
    pallas_call x1, Pallas kernels, local(): pl.pallas_call(hand_on, name='hand_on', out_shape=out_shape, in_specs=[an...  2.76 us

profile of v2, /device:TPU:1, one launch (start us, length us, event | category | flops | bytes accessed | tf_op | source)
XLA Modules:
  0.0 106.6 jit_solution(5049825145248372453)
XLA Ops:
  0.6 103.2 %triangle.1 = (bf16[16,256,128]{2,1,0:T(8,128)(2,1)}, bf16[16,256,128]{2,1,0:T(8,128)(2,1)}, f32[128,640]{1,0:T(8,128)}, f32[128,128]{1,0:T(8,128)}, f32[1,128]{1,0:T(1,128)}, /*index=5*/f32[1,128]{1,0:T(1,128)}) custom-call(bf16[16,256,128]{2,1,0:T(8,128)(2,1)} %bitcast.8, bf16[16,256,128]{2,1,0:T(8,128)(2,1)} %bitcast.9, bf16[128,640]{1,0:T(8,128)(2,1)} %w_in_h.1, ...), custom_call_target="tpu_custom_call" | custom-call | flops 3300000000 | bytes 5000000 | tf_op jit(solution)/shard_map/triangle/pallas_call | solution.py:435
  103.9 2.8 %hand_on.1 = (bf16[16,256,128]{2,1,0:T(8,128)(2,1)}, bf16[16,256,128]{2,1,0:T(8,128)(2,1)}, f32[128,640]{1,0:T(8,128)}, f32[128,128]{1,0:T(8,128)}, f32[1,128]{1,0:T(1,128)}, /*index=5*/f32[1,128]{1,0:T(1,128)}) custom-call(bf16[16,256,128]{2,1,0:T(8,128)(2,1)} %get-tuple-element.18.refs_0_, bf16[16,256,128]{2,1,0:T(8,128)(2,1)} %get-tuple-element.19.refs_1_, ...), custom_call_target="tpu_custom_call" | custom-call | tf_op jit(solution)/shard_map/hand_on/pallas_call | solution.py:486

commit v3 on v2

--- a/solution.py
+++ b/solution.py
@@ -10,6 +10,7 @@
 MESH = pl.DeviceIdType.MESH
 F32 = jnp.float32
 BF16 = jnp.bfloat16
+UNROLL = 2
 LEFT, RIGHT, PROD, GPROD, GLEFT, GRIGHT = range(6)
 
 
@@ -39,12 +40,12 @@
 def kernel(
     n_dp, n_ax, factor,
     pair_h, cot_h, w_in_h, w_out_h, gain_in_h, gain_x_h,
-    upd_h, gpair_h, gw_in_h, gw_out_h, ggi_h, ggx_h,
+    upd_h, gpair_h, fin,
     pair, cot, w_in, w_out, gain_in, gain_x,
-    upd, gpair, gw_in, gw_out, ggi, ggx, isem, osem, gproj,
+    upd, gpair, isem, osem, fsem, gproj,
     send, recv, tbuf, tbuf2, lc, rc, gc,
     normed, unit_in, inv_in, gate_a, q_a, gate_b, q_b, gate_o, s_x, c_g, glift, xnorm, gnorm,
-    w_t, wo_t, gin, gx, dw, r1, r2, s1, s2, fin,
+    w_t, wo_t, gin, gx, dw, r1, r2, s1, s2,
     ssem, rsem, lsem, asend, arecv,
 ):
     me = lax.axis_index("axial")
@@ -57,7 +58,7 @@
     def dp_peer(o):
         return (dp + o) % n_dp
 
-    def each(lo, hi, fn, unroll=1):
+    def each(lo, hi, fn, unroll=UNROLL):
         def body(i, carry):
             fn(i)
             return carry
@@ -78,7 +79,6 @@
     out_pairs = {
         "upd": (upd, upd_h),
         "gpair0": (gpair.at[half[0]], gpair_h.at[half[0]]), "gpair1": (gpair.at[half[1]], gpair_h.at[half[1]]),
-        "gw_in": (gw_in, gw_in_h), "gw_out": (gw_out, gw_out_h), "ggi": (ggi, ggi_h), "ggx": (ggx, ggx_h),
     }
     in_names, put_names = list(in_pairs), list(out_pairs)
 
@@ -145,7 +145,7 @@
         pltpu.make_async_copy(part, part, arecv.at[3 + p]).wait()
         total = jnp.sum(r2[p], axis=0) * factor
         s2[p] = total
-        fin[p, me] = total
+        pltpu.make_async_copy(s2.at[p], fin.at[p, me], fsem.at[p]).start()
 
         def one(o):
             pltpu.make_async_remote_copy(
@@ -157,6 +157,7 @@
     def reduce_end(p):
         part = fin.at[p, pl.ds(0, n_ax - 1)]
         pltpu.make_async_copy(part, part, arecv.at[6 + p]).wait()
+        pltpu.make_async_copy(s2.at[p], fin.at[p, me], fsem.at[p]).wait()
 
     def reduce_sent(p):
         part = r1.at[p, pl.ds(0, n_ax - 1)]
@@ -335,27 +336,28 @@
     start(2 * GRIGHT + 1)
     put_out("upd")
 
-    def back_row(k, h, p, gate_ref, q_ref):
-        i = 8 * h + k
-        grad = take(k)
-        both = jnp.concatenate([grad * gate_ref[i], grad * q_ref[i]], axis=0).astype(BF16)
-        gproj[k] = both
-        dw[p] += dot_nt(normed[i], both)
-
     def back_a(h):
         def grad_row(k):
-            back_row(k, h, 1, gate_a, q_a)
-            gnorm[8 * h + k] += dot(w_in[:, 0:256], gproj[k])
+            i = 8 * h + k
+            grad = take(k)
+            both = jnp.concatenate([grad * gate_a[i], grad * q_a[i]], axis=0).astype(BF16)
+            dw[1] += dot_nt(normed[i], both)
+            gnorm[i] += dot(w_in[:, 0:256], both)
         wait_recv(2 * GLEFT + h)
         unpack(2 * GLEFT + h)
         each(0, 8, grad_row)
 
     def back_b(h):
-        def grad_row(k):
-            back_row(k, h, 2, gate_b, q_b)
         wait_recv(2 * GRIGHT + h)
         unpack(2 * GRIGHT + h)
-        each(0, 8, grad_row)
+        total = dw[2]
+        for k in range(8):
+            i = 8 * h + k
+            grad = take(k)
+            both = jnp.concatenate([grad * gate_b[i], grad * q_b[i]], axis=0).astype(BF16)
+            gproj[k] = both
+            total += dot_nt(normed[i], both)
+        dw[2] = total
 
     def out_rows(h):
         def out_row(k):
@@ -377,44 +379,54 @@
     back_b(1)
     reduce_start(2)
     reduce_dp(1)
+    reduce_back(0)
     out_rows(1)
     reduce_dp(2)
-    reduce_back(0)
     reduce_back(1)
-    reduce_end(0)
-    reduce_end(1)
-    first = fin[0].reshape(128, 256)
-    gw_out[...] = first[:, :128]
-    gw_in[:, 512:640] = first[:, 128:]
-    gw_in[:, 0:256] = fin[1].reshape(128, 256)
-    row_x = jnp.sum(first[:, :128] * w_out[...].astype(F32), axis=1, keepdims=True)
-    ggx[...] = jnp.broadcast_to(row_x, (128, 128)).T[:1] / gain_x[...]
     reduce_back(2)
     for t in range(12):
         wait_send(t)
+    for name in put_names:
+        out_copy(name).wait()
     for p in range(3):
         reduce_sent(p)
-    reduce_end(2)
-    gw_in[:, 256:512] = fin[2].reshape(128, 256)
+    for p in range(3):
+        reduce_end(p)
+
+
+def hand_on(
+    upd_h, gpair_h, fin_h, w_in_h, w_out_h, gain_in_h, gain_x_h,
+    upd_o, gpair_o, gw_in_o, gw_out_o, ggi_o, ggx_o,
+    upd, gpair, gw_in, gw_out, ggi, ggx, fin, w_in, w_out, gain_in, gain_x, isem, osem,
+):
+    def moves(pairs, sems, first):
+        return [pltpu.make_async_copy(a, b, sems.at[first + n]) for n, (a, b) in enumerate(pairs)]
+
+    small_in = moves(((fin_h, fin), (w_in_h, w_in), (w_out_h, w_out), (gain_in_h, gain_in),
+                      (gain_x_h, gain_x)), isem, 0)
+    big_in = moves(((upd_h, upd), (gpair_h, gpair)), isem, 5)
+    big_out = moves(((upd, upd_o), (gpair, gpair_o)), osem, 0)
+    small_out = moves(((gw_in, gw_in_o), (gw_out, gw_out_o), (ggi, ggi_o), (ggx, ggx_o)), osem, 2)
+    for copy in small_in + big_in:
+        copy.start()
+    for copy in small_in:
+        copy.wait()
+    gw_out[...] = fin[0, :, 0:128]
+    gw_in[:, 512:640] = fin[0, :, 128:256]
+    gw_in[:, 0:256] = fin[1]
+    gw_in[:, 256:512] = fin[2]
+    small_out[0].start()
+    small_out[1].start()
+    for n in range(2):
+        big_in[n].wait()
+        big_out[n].start()
+    row_x = jnp.sum(gw_out[...] * w_out[...].astype(F32), axis=1, keepdims=True)
+    ggx[...] = jnp.broadcast_to(row_x, (128, 128)).T[:1] / gain_x[...]
     row_in = jnp.sum(gw_in[...] * w_in[...].astype(F32), axis=1, keepdims=True)
     ggi[...] = jnp.broadcast_to(row_in, (128, 128)).T[:1] / gain_in[...]
-    for name in ("gw_in", "gw_out", "ggi", "ggx"):
-        put_out(name)
-    for name in put_names:
-        out_copy(name).wait()
-
-
-def hand_on(*refs):
-    n = 6
-    sources, targets, held, sems = refs[:n], refs[n:2 * n], refs[2 * n:3 * n], refs[3 * n]
-    ins = [pltpu.make_async_copy(sources[k], held[k], sems.at[k]) for k in range(n)]
-    outs = [pltpu.make_async_copy(held[k], targets[k], sems.at[n + k]) for k in range(n)]
-    for copy in ins:
-        copy.start()
-    for k in range(n):
-        ins[k].wait()
-        outs[k].start()
-    for copy in outs:
+    small_out[2].start()
+    small_out[3].start()
+    for copy in big_out + small_out:
         copy.wait()
 
 
@@ -432,15 +444,17 @@
         jax.ShapeDtypeStruct((1, 128), F32),
         jax.ShapeDtypeStruct((1, 128), F32),
     )
-    outs = pl.pallas_call(
+    sums_shape = jax.ShapeDtypeStruct((3, 16, 8, 256), F32)
+    upd, gpair, sums = pl.pallas_call(
         functools.partial(kernel, n_dp, n_ax, factor),
         name="triangle",
-        out_shape=out_shape,
-        in_specs=[pl.BlockSpec(memory_space=pltpu.HBM)] * 6,
-        out_specs=(anywhere,) * 6,
-        scratch_shapes=[pltpu.VMEM(v.shape, v.dtype) for v in args + out_shape] + [
+        out_shape=out_shape[:2] + (sums_shape,),
+        in_specs=[anywhere] * 6,
+        out_specs=(anywhere,) * 3,
+        scratch_shapes=[pltpu.VMEM(v.shape, v.dtype) for v in args + out_shape[:2]] + [
             pltpu.SemaphoreType.DMA((7,)),
-            pltpu.SemaphoreType.DMA((7,)),
+            pltpu.SemaphoreType.DMA((3,)),
+            pltpu.SemaphoreType.DMA((3,)),
             pltpu.VMEM((8, 256, 256), BF16),
             pltpu.VMEM((12, 16, 64, 256), BF16),
             pltpu.VMEM((12, 16, 64, 256), BF16),
@@ -471,7 +485,6 @@
             pltpu.VMEM((3, 8, 8, 256), F32),
             pltpu.VMEM((3, 8, 256), F32),
             pltpu.VMEM((3, 8, 256), F32),
-            pltpu.VMEM((3, 16, 8, 256), F32),
             pltpu.SemaphoreType.DMA((12,)),
             pltpu.SemaphoreType.DMA((12,)),
             pltpu.SemaphoreType.DMA((12,)),
@@ -487,12 +500,15 @@
         hand_on,
         name="hand_on",
         out_shape=out_shape,
-        in_specs=[anywhere] * 6,
+        in_specs=[anywhere] * 7,
         out_specs=(anywhere,) * 6,
         scratch_shapes=[pltpu.VMEM(v.shape, v.dtype) for v in out_shape] + [
-            pltpu.SemaphoreType.DMA((12,))],
+            pltpu.VMEM((3, 128, 256), F32)] + [pltpu.VMEM(v.shape, v.dtype) for v in args[2:]] + [
+            pltpu.SemaphoreType.DMA((7,)),
+            pltpu.SemaphoreType.DMA((6,)),
+        ],
         compiler_params=pltpu.CompilerParams(vmem_limit_bytes=60 * 2**20),
-    )(*outs)
+    )(upd, gpair, sums.reshape(3, 128, 256), *args[2:])
     return upd[None], gpair[None], gw_in, gw_out, ggi[0], ggx[0]
 
 

time: 107 us -> 103 us (0.963)
  Pallas kernels: 106 us -> 102 us
    pallas_call x1, Pallas kernels: 103 us -> 98.8 us  [local(): pl.pallas_call(functools.partial(kernel, n_dp, n_ax, factor), name='trian...]
where the time goes in v3:
time: 103 us; the launch traced here: 102 us
  Pallas kernels  102 us (99%)
    pallas_call x1, Pallas kernels, local(): pl.pallas_call(functools.partial(kernel, n_dp, n_ax, factor), name='trian...  98.8 us
    pallas_call x1, Pallas kernels, local(): pl.pallas_call(hand_on, name='hand_on', out_shape=out_shape, in_specs=[an...  2.92 us

profile of v3, /device:TPU:1, one launch (start us, length us, event | category | flops | bytes accessed | tf_op | source)
XLA Modules:
  0.0 102.4 jit_solution(14533990106874368477)
XLA Ops:
  0.6 98.8 %triangle.1 = (bf16[16,256,128]{2,1,0:T(8,128)(2,1)}, bf16[16,256,128]{2,1,0:T(8,128)(2,1)}, f32[3,16,8,256]{3,2,1,0:T(8,128)}) custom-call(bf16[16,256,128]{2,1,0:T(8,128)(2,1)} %bitcast.14, bf16[16,256,128]{2,1,0:T(8,128)(2,1)} %bitcast.15, bf16[128,640]{1,0:T(8,128)(2,1)} %w_in_h.3, bf16[128,128]{1,0:T(8,128)(2,1)} %w_out_h.3, f32[1,128]{1,0:T(1,128)} %bitcast.10, ...), custom_call_target="tpu_custom_call" | custom-call | flops 3300000000 | bytes 5000000 | tf_op jit(solution)/shard_map/triangle/pallas_call | solution.py:448
  99.5 2.9 %hand_on.1 = (bf16[16,256,128]{2,1,0:T(8,128)(2,1)}, bf16[16,256,128]{2,1,0:T(8,128)(2,1)}, f32[128,640]{1,0:T(8,128)}, f32[128,128]{1,0:T(8,128)}, f32[1,128]{1,0:T(1,128)}, /*index=5*/f32[1,128]{1,0:T(1,128)}) custom-call(bf16[16,256,128]{2,1,0:T(8,128)(2,1)} %get-tuple-element.15.upd_h, bf16[16,256,128]{2,1,0:T(8,128)(2,1)} %get-tuple-element.16.gpair_h, ...), custom_call_target="tpu_custom_call" | custom-call | tf_op jit(solution)/shard_map/hand_on/pallas_call | solution.py:499

commit v4 on v3

--- a/solution.py
+++ b/solution.py
@@ -45,7 +45,7 @@
     upd, gpair, isem, osem, fsem, gproj,
     send, recv, tbuf, tbuf2, lc, rc, gc,
     normed, unit_in, inv_in, gate_a, q_a, gate_b, q_b, gate_o, s_x, c_g, glift, xnorm, gnorm,
-    w_t, wo_t, gin, gx, dw, r1, r2, s1, s2,
+    w_t, wo_t, gin, gx, dw, r1, r2, s1, s2, x1, xs, a1, a2, s3, s4, xg,
     ssem, rsem, lsem, asend, arecv,
 ):
     me = lax.axis_index("axial")
@@ -116,56 +116,99 @@
         part = send.at[t, pl.ds(0, n_ax - 1)]
         pltpu.make_async_copy(part, part, ssem.at[t]).wait()
 
-    def reduce_start(p):
+    def bytes_of(ref, sem):
+        pltpu.make_async_copy(ref, ref, sem).wait()
+
+    def push(src, dst, k, dp_index, ax_index):
+        pltpu.make_async_remote_copy(
+            src_ref=src, dst_ref=dst, send_sem=asend.at[k], recv_sem=arecv.at[k],
+            device_id=(dp_index, ax_index), device_id_type=MESH).start()
+
+    def rows8(n):
+        return pl.ds(pl.multiple_of(8 * n, 8), 8)
+
+    def rows32(n):
+        return pl.ds(pl.multiple_of(32 * n, 32), 32)
+
+    right_blocks = pl.ds(4, 2)
+    others = pl.ds(0, n_ax - 1)
+
+    def right_start():
         def one(o):
             d = peer(o)
-            pltpu.make_async_remote_copy(
-                src_ref=dw.at[p, pl.ds(8 * d, 8)], dst_ref=r1.at[p, me],
-                send_sem=asend.at[p], recv_sem=arecv.at[p],
-                device_id=(dp, d), device_id_type=MESH).start()
+            push(dw.at[right_blocks, rows8(d)], r1.at[me], 0, dp, d)
         each(1, n_ax, one)
-        r1[p, me] = dw[p, pl.ds(8 * me, 8)]
-
-    def reduce_dp(p):
-        part = r1.at[p, pl.ds(0, n_ax - 1)]
-        pltpu.make_async_copy(part, part, arecv.at[p]).wait()
-        total = jnp.sum(r1[p], axis=0)
-        s1[p] = total
-        r2[p, dp] = total
-
+        r1[me] = dw[4:6, rows8(me)]
+
+    def right_dp():
+        bytes_of(r1.at[others], arecv.at[0])
+        total = jnp.sum(r1[...], axis=0)
+        s1[...] = total
+        r2[dp] = total
+        each(1, n_dp, lambda o: push(s1, r2.at[dp], 1, dp_peer(o), me))
+
+    def right_back():
+        bytes_of(r2.at[pl.ds(0, n_dp - 1)], arecv.at[1])
+        s2[...] = jnp.sum(r2[...], axis=0) * factor
+        target = fin.at[right_blocks, rows8(me)]
+        pltpu.make_async_copy(s2, target, fsem.at[0]).start()
+        each(1, n_ax, lambda o: push(s2, target, 2, dp, peer(o)))
+
+    my_x, my_yl = dp % 4, dp // 4
+
+    def x_peer(o):
+        return my_yl * 4 + (my_x + o) % 4
+
+    def x_start(p):
         def one(o):
-            pltpu.make_async_remote_copy(
-                src_ref=s1.at[p], dst_ref=r2.at[p, dp],
-                send_sem=asend.at[3 + p], recv_sem=arecv.at[3 + p],
-                device_id=(dp_peer(o), me), device_id_type=MESH).start()
-        each(1, n_dp, one)
-
-    def reduce_back(p):
-        part = r2.at[p, pl.ds(0, n_dp - 1)]
-        pltpu.make_async_copy(part, part, arecv.at[3 + p]).wait()
-        total = jnp.sum(r2[p], axis=0) * factor
-        s2[p] = total
-        pltpu.make_async_copy(s2.at[p], fin.at[p, me], fsem.at[p]).start()
+            push(dw.at[pl.ds(2 * p, 2), rows32((my_x + o) % 4)], x1.at[p, my_x], 3 + p, x_peer(o), me)
+        each(1, 4, one)
+        x1[p, my_x] = dw[2 * p:2 * p + 2, rows32(my_x)]
+
+    def left_axial():
+        for p in range(2):
+            bytes_of(x1.at[p, pl.ds(0, 3)], arecv.at[3 + p])
+            xs[2 * p:2 * p + 2] = jnp.sum(x1[p], axis=0)
 
         def one(o):
-            pltpu.make_async_remote_copy(
-                src_ref=s2.at[p], dst_ref=fin.at[p, me],
-                send_sem=asend.at[6 + p], recv_sem=arecv.at[6 + p],
-                device_id=(dp, peer(o)), device_id_type=MESH).start()
+            d = peer(o)
+            push(xs.at[d // 4, rows8(d % 4)], a1.at[me], 5, dp, d)
         each(1, n_ax, one)
-
-    def reduce_end(p):
-        part = fin.at[p, pl.ds(0, n_ax - 1)]
-        pltpu.make_async_copy(part, part, arecv.at[6 + p]).wait()
-        pltpu.make_async_copy(s2.at[p], fin.at[p, me], fsem.at[p]).wait()
-
-    def reduce_sent(p):
-        part = r1.at[p, pl.ds(0, n_ax - 1)]
-        pltpu.make_async_copy(part, part, asend.at[p]).wait()
-        part = r2.at[p, pl.ds(0, n_dp - 1)]
-        pltpu.make_async_copy(part, part, asend.at[3 + p]).wait()
-        part = fin.at[p, pl.ds(0, n_ax - 1)]
-        pltpu.make_async_copy(part, part, asend.at[6 + p]).wait()
+        a1[me] = xs[me // 4, rows8(me % 4)]
+
+    def left_y():
+        bytes_of(a1.at[others], arecv.at[5])
+        total = jnp.sum(a1[...], axis=0)
+        s3[...] = total
+        a2[my_yl] = total
+        push(s3, a2.at[my_yl], 6, (dp + 4) % 8, me)
+
+    def left_back():
+        bytes_of(a2.at[0], arecv.at[6])
+        total = (a2[0] + a2[1]) * factor
+        s4[...] = total
+        xg[me // 4, rows8(me % 4)] = total
+        each(1, n_ax, lambda o: push(s4, xg.at[me // 4, rows8(me % 4)], 7, dp, peer(o)))
+
+    def left_x():
+        bytes_of(a1.at[others], arecv.at[7])
+        target = fin.at[pl.ds(0, 4), rows32(my_x)]
+        pltpu.make_async_copy(xg, target, fsem.at[1]).start()
+        each(1, 4, lambda o: push(xg, target, 8, x_peer(o), me))
+
+    def reduce_end():
+        for sem in (asend, arecv):
+            bytes_of(fin.at[right_blocks, pl.ds(0, 8 * (n_ax - 1))], sem.at[2])
+            bytes_of(fin.at[pl.ds(0, 4), pl.ds(0, 96)], sem.at[8])
+        bytes_of(r1.at[others], asend.at[0])
+        bytes_of(r2.at[pl.ds(0, n_dp - 1)], asend.at[1])
+        for p in range(2):
+            bytes_of(x1.at[p, pl.ds(0, 3)], asend.at[3 + p])
+        bytes_of(a1.at[others], asend.at[5])
+        bytes_of(a2.at[0], asend.at[6])
+        bytes_of(a1.at[others], asend.at[7])
+        pltpu.make_async_copy(s2, fin.at[right_blocks, rows8(me)], fsem.at[0]).wait()
+        pltpu.make_async_copy(xg, fin.at[pl.ds(0, 4), rows32(my_x)], fsem.at[1]).wait()
 
     def strided(i):
         return pl.ds(i, 128, stride=8)
@@ -306,8 +349,8 @@
         lifted = dot(wo_t[...], flat)
         upd[i] = (gate_o[i] * lifted).T.astype(BF16)
         ggate = (lifted * c_g[i]).astype(BF16)
-        dw[0, :, 0:128] += dot_nt(flat, glift[i])
-        dw[0, :, 128:256] += dot_nt(normed[i], ggate)
+        dw[0] += dot_nt(flat, glift[i])
+        dw[1] += dot_nt(normed[i], ggate)
         gnorm[i] = dot(w_in[:, 512:640], ggate)
 
     for h in range(2):
@@ -325,7 +368,7 @@
         start(2 * GLEFT + h)
         each(8 * h, 8 * h + 8, lift_row)
 
-    reduce_start(0)
+    x_start(0)
 
     def gright_pair(cp):
         outs = [dot_tn(gc[2 * cp + e], lc[2 * cp + e]).reshape(16, 2, 8, 256) for e in range(2)]
@@ -341,7 +384,9 @@
             i = 8 * h + k
             grad = take(k)
             both = jnp.concatenate([grad * gate_a[i], grad * q_a[i]], axis=0).astype(BF16)
-            dw[1] += dot_nt(normed[i], both)
+            local = dot_nt(normed[i], both)
+            dw[2] += local[:, :128]
+            dw[3] += local[:, 128:]
             gnorm[i] += dot(w_in[:, 0:256], both)
         wait_recv(2 * GLEFT + h)
         unpack(2 * GLEFT + h)
@@ -350,14 +395,15 @@
     def back_b(h):
         wait_recv(2 * GRIGHT + h)
         unpack(2 * GRIGHT + h)
-        total = dw[2]
+        total = jnp.concatenate([dw[4], dw[5]], axis=1)
         for k in range(8):
             i = 8 * h + k
             grad = take(k)
             both = jnp.concatenate([grad * gate_b[i], grad * q_b[i]], axis=0).astype(BF16)
             gproj[k] = both
             total += dot_nt(normed[i], both)
-        dw[2] = total
+        dw[4] = total[:, :128]
+        dw[5] = total[:, 128:]
 
     def out_rows(h):
         def out_row(k):
@@ -372,26 +418,23 @@
 
     back_a(0)
     back_a(1)
-    reduce_start(1)
+    x_start(1)
     back_b(0)
-    reduce_dp(0)
+    left_axial()
     out_rows(0)
     back_b(1)
-    reduce_start(2)
-    reduce_dp(1)
-    reduce_back(0)
+    right_start()
+    left_y()
     out_rows(1)
-    reduce_dp(2)
-    reduce_back(1)
-    reduce_back(2)
+    left_back()
+    right_dp()
+    left_x()
+    right_back()
     for t in range(12):
         wait_send(t)
     for name in put_names:
         out_copy(name).wait()
-    for p in range(3):
-        reduce_sent(p)
-    for p in range(3):
-        reduce_end(p)
+    reduce_end()
 
 
 def hand_on(
@@ -404,20 +447,21 @@
 
     small_in = moves(((fin_h, fin), (w_in_h, w_in), (w_out_h, w_out), (gain_in_h, gain_in),
                       (gain_x_h, gain_x)), isem, 0)
-    big_in = moves(((upd_h, upd), (gpair_h, gpair)), isem, 5)
-    big_out = moves(((upd, upd_o), (gpair, gpair_o)), osem, 0)
-    small_out = moves(((gw_in, gw_in_o), (gw_out, gw_out_o), (ggi, ggi_o), (ggx, ggx_o)), osem, 2)
+    halves = pl.ds(0, 8), pl.ds(8, 8)
+    big_in = moves([(a.at[h], b.at[h]) for a, b in ((upd_h, upd), (gpair_h, gpair)) for h in halves], isem, 5)
+    big_out = moves([(a.at[h], b.at[h]) for a, b in ((upd, upd_o), (gpair, gpair_o)) for h in halves], osem, 0)
+    small_out = moves(((gw_in, gw_in_o), (gw_out, gw_out_o), (ggi, ggi_o), (ggx, ggx_o)), osem, 4)
     for copy in small_in + big_in:
         copy.start()
     for copy in small_in:
         copy.wait()
-    gw_out[...] = fin[0, :, 0:128]
-    gw_in[:, 512:640] = fin[0, :, 128:256]
-    gw_in[:, 0:256] = fin[1]
-    gw_in[:, 256:512] = fin[2]
+    gw_out[...] = fin[0]
+    gw_in[:, 512:640] = fin[1]
+    for n in range(4):
+        gw_in[:, 128 * n:128 * (n + 1)] = fin[2 + n]
     small_out[0].start()
     small_out[1].start()
-    for n in range(2):
+    for n in range(4):
         big_in[n].wait()
         big_out[n].start()
     row_x = jnp.sum(gw_out[...] * w_out[...].astype(F32), axis=1, keepdims=True)
@@ -444,7 +488,7 @@
         jax.ShapeDtypeStruct((1, 128), F32),
         jax.ShapeDtypeStruct((1, 128), F32),
     )
-    sums_shape = jax.ShapeDtypeStruct((3, 16, 8, 256), F32)
+    sums_shape = jax.ShapeDtypeStruct((6, 128, 128), F32)
     upd, gpair, sums = pl.pallas_call(
         functools.partial(kernel, n_dp, n_ax, factor),
         name="triangle",
@@ -454,7 +498,7 @@
         scratch_shapes=[pltpu.VMEM(v.shape, v.dtype) for v in args + out_shape[:2]] + [
             pltpu.SemaphoreType.DMA((7,)),
             pltpu.SemaphoreType.DMA((3,)),
-            pltpu.SemaphoreType.DMA((3,)),
+            pltpu.SemaphoreType.DMA((2,)),
             pltpu.VMEM((8, 256, 256), BF16),
             pltpu.VMEM((12, 16, 64, 256), BF16),
             pltpu.VMEM((12, 16, 64, 256), BF16),
@@ -480,11 +524,18 @@
             pltpu.VMEM((128, 128), BF16),
             pltpu.VMEM((128, 256), F32),
             pltpu.VMEM((128, 256), F32),
-            pltpu.VMEM((3, 128, 256), F32),
-            pltpu.VMEM((3, 16, 8, 256), F32),
-            pltpu.VMEM((3, 8, 8, 256), F32),
-            pltpu.VMEM((3, 8, 256), F32),
-            pltpu.VMEM((3, 8, 256), F32),
+            pltpu.VMEM((6, 128, 128), F32),
+            pltpu.VMEM((16, 2, 8, 128), F32),
+            pltpu.VMEM((8, 2, 8, 128), F32),
+            pltpu.VMEM((2, 8, 128), F32),
+            pltpu.VMEM((2, 8, 128), F32),
+            pltpu.VMEM((2, 4, 2, 32, 128), F32),
+            pltpu.VMEM((4, 32, 128), F32),
+            pltpu.VMEM((16, 8, 128), F32),
+            pltpu.VMEM((2, 8, 128), F32),
+            pltpu.VMEM((8, 128), F32),
+            pltpu.VMEM((8, 128), F32),
+            pltpu.VMEM((4, 32, 128), F32),
             pltpu.SemaphoreType.DMA((12,)),
             pltpu.SemaphoreType.DMA((12,)),
             pltpu.SemaphoreType.DMA((12,)),
@@ -503,12 +554,12 @@
         in_specs=[anywhere] * 7,
         out_specs=(anywhere,) * 6,
         scratch_shapes=[pltpu.VMEM(v.shape, v.dtype) for v in out_shape] + [
-            pltpu.VMEM((3, 128, 256), F32)] + [pltpu.VMEM(v.shape, v.dtype) for v in args[2:]] + [
-            pltpu.SemaphoreType.DMA((7,)),
-            pltpu.SemaphoreType.DMA((6,)),
+            pltpu.VMEM((6, 128, 128), F32)] + [pltpu.VMEM(v.shape, v.dtype) for v in args[2:]] + [
+            pltpu.SemaphoreType.DMA((9,)),
+            pltpu.SemaphoreType.DMA((8,)),
         ],
         compiler_params=pltpu.CompilerParams(vmem_limit_bytes=60 * 2**20),
-    )(upd, gpair, sums.reshape(3, 128, 256), *args[2:])
+    )(upd, gpair, sums, *args[2:])
     return upd[None], gpair[None], gw_in, gw_out, ggi[0], ggx[0]
 
 

time: 103 us -> 100 us (0.971)
  Pallas kernels: 102 us -> 99.7 us
    pallas_call x1, Pallas kernels: 98.8 us -> 96.9 us  [local(): pl.pallas_call(functools.partial(kernel, n_dp, n_ax, factor), name='trian...]
where the time goes in v4:
time: 100 us
  Pallas kernels  99.7 us (100%)
    pallas_call x1, Pallas kernels, local(): pl.pallas_call(functools.partial(kernel, n_dp, n_ax, factor), name='trian...  96.9 us
    pallas_call x1, Pallas kernels, local(): pl.pallas_call(hand_on, name='hand_on', out_shape=out_shape, in_specs=[an...  2.76 us

profile of v4, /device:TPU:1, one launch (start us, length us, event | category | flops | bytes accessed | tf_op | source)
XLA Modules:
  0.0 100.3 jit_solution(1052474752342362577)
XLA Ops:
  0.6 96.9 %triangle.1 = (bf16[16,256,128]{2,1,0:T(8,128)(2,1)}, bf16[16,256,128]{2,1,0:T(8,128)(2,1)}, f32[6,128,128]{2,1,0:T(8,128)}) custom-call(bf16[16,256,128]{2,1,0:T(8,128)(2,1)} %bitcast.12, bf16[16,256,128]{2,1,0:T(8,128)(2,1)} %bitcast.13, bf16[128,640]{1,0:T(8,128)(2,1)} %w_in_h.3, bf16[128,128]{1,0:T(8,128)(2,1)} %w_out_h.3, f32[1,128]{1,0:T(1,128)} %bitcast.8, ...), custom_call_target="tpu_custom_call" | custom-call | flops 3300000000 | bytes 5000000 | tf_op jit(solution)/shard_map/triangle/pallas_call | solution.py:492
  97.5 2.8 %hand_on.1 = (bf16[16,256,128]{2,1,0:T(8,128)(2,1)}, bf16[16,256,128]{2,1,0:T(8,128)(2,1)}, f32[128,640]{1,0:T(8,128)}, f32[128,128]{1,0:T(8,128)}, f32[1,128]{1,0:T(1,128)}, /*index=5*/f32[1,128]{1,0:T(1,128)}) custom-call(bf16[16,256,128]{2,1,0:T(8,128)(2,1)} %get-tuple-element.15.upd_h, bf16[16,256,128]{2,1,0:T(8,128)(2,1)} %get-tuple-element.16.gpair_h, ...), custom_call_target="tpu_custom_call" | custom-call | tf_op jit(solution)/shard_map/hand_on/pallas_call | solution.py:550

commit v5 on v4

--- a/solution.py
+++ b/solution.py
@@ -101,11 +101,41 @@
         def one(o):
             d = peer(o)
             pltpu.make_async_remote_copy(
-                src_ref=send.at[t, d], dst_ref=recv.at[t, me],
+                src_ref=send.at[t, d, part], dst_ref=recv.at[t, me, part],
                 send_sem=ssem.at[t], recv_sem=rsem.at[t],
                 device_id=(dp, d), device_id_type=MESH).start()
+        for q in range(2):
+            part = pl.ds(32 * q, 32)
+            each(1, n_ax, one)
+        pltpu.make_async_copy(send.at[t, me], recv.at[t, me], lsem.at[t]).start()
+
+    last = 2 * GRIGHT + 1
+
+    def lanes(n):
+        return slice(128 * n, 128 * (n + 1))
+
+    def last_copy(n):
+        return pltpu.make_async_copy(
+            send.at[last, me, :, lanes(n)], recv.at[last, me, :, lanes(n)], lsem.at[last + n])
+
+    def start_last(n):
+        def one(o):
+            d = peer(o)
+            pltpu.make_async_remote_copy(
+                src_ref=send.at[last, d, :, lanes(n)], dst_ref=recv.at[last, me, :, lanes(n)],
+                send_sem=ssem.at[last + n], recv_sem=rsem.at[last + n],
+                device_id=(dp, d), device_id_type=MESH).start()
         each(1, n_ax, one)
-        pltpu.make_async_copy(send.at[t, me], recv.at[t, me], lsem.at[t]).start()
+        last_copy(n).start()
+
+    def wait_last(n):
+        last_copy(n).wait()
+        part = recv.at[last, pl.ds(0, n_ax - 1), :, lanes(n)]
+        pltpu.make_async_copy(part, part, rsem.at[last + n]).wait()
+
+    def wait_last_sent(n):
+        part = send.at[last, pl.ds(0, n_ax - 1), :, lanes(n)]
+        pltpu.make_async_copy(part, part, ssem.at[last + n]).wait()
 
     def wait_recv(t):
         pltpu.make_async_copy(send.at[t, me], recv.at[t, me], lsem.at[t]).wait()
@@ -376,7 +406,8 @@
             store_pair(2 * GRIGHT + h, cp, outs[0][:, h], outs[1][:, h])
     each(0, 4, gright_pair)
     start(2 * GRIGHT)
-    start(2 * GRIGHT + 1)
+    start_last(0)
+    start_last(1)
     put_out("upd")
 
     def back_a(h):
@@ -393,15 +424,25 @@
         each(0, 8, grad_row)
 
     def back_b(h):
-        wait_recv(2 * GRIGHT + h)
-        unpack(2 * GRIGHT + h)
         total = jnp.concatenate([dw[4], dw[5]], axis=1)
-        for k in range(8):
-            i = 8 * h + k
-            grad = take(k)
-            both = jnp.concatenate([grad * gate_b[i], grad * q_b[i]], axis=0).astype(BF16)
-            gproj[k] = both
-            total += dot_nt(normed[i], both)
+        if h == 0:
+            wait_recv(2 * GRIGHT)
+        for n in range(2):
+            if h == 1:
+                wait_last(n)
+            tbuf[n] = recv[2 * GRIGHT + h, :, :, lanes(n)].astype(F32).reshape(1024, 128)
+            for k in range(0, 8, 2):
+                sides = []
+                for e in (k, k + 1):
+                    i = 8 * h + e
+                    grad = tbuf[n, strided(e), :]
+                    both = jnp.concatenate(
+                        [grad * gate_b[i, :, lanes(n)], grad * q_b[i, :, lanes(n)]], axis=0).astype(BF16)
+                    gproj[e, :, lanes(n)] = both
+                    sides.append((normed[i, :, lanes(n)], both))
+                total += dot_nt(
+                    jnp.concatenate([sides[0][0], sides[1][0]], axis=1),
+                    jnp.concatenate([sides[0][1], sides[1][1]], axis=1))
         dw[4] = total[:, :128]
         dw[5] = total[:, 128:]
 
@@ -430,8 +471,10 @@
     right_dp()
     left_x()
     right_back()
-    for t in range(12):
+    for t in range(11):
         wait_send(t)
+    for n in range(2):
+        wait_last_sent(n)
     for name in put_names:
         out_copy(name).wait()
     reduce_end()
@@ -536,9 +579,9 @@
             pltpu.VMEM((8, 128), F32),
             pltpu.VMEM((8, 128), F32),
             pltpu.VMEM((4, 32, 128), F32),
-            pltpu.SemaphoreType.DMA((12,)),
-            pltpu.SemaphoreType.DMA((12,)),
-            pltpu.SemaphoreType.DMA((12,)),
+            pltpu.SemaphoreType.DMA((13,)),
+            pltpu.SemaphoreType.DMA((13,)),
+            pltpu.SemaphoreType.DMA((13,)),
             pltpu.SemaphoreType.DMA((9,)),
             pltpu.SemaphoreType.DMA((9,)),
         ],

time: 100 us -> 99.6 us (level)
  no operation moved by 1% of the time
where the time goes in v5:
time: 99.6 us; the launch traced here: 99.5 us
  Pallas kernels  98.8 us (99%)
    pallas_call x1, Pallas kernels, local(): pl.pallas_call(functools.partial(kernel, n_dp, n_ax, factor), name='trian...  96.1 us
    pallas_call x1, Pallas kernels, local(): pl.pallas_call(hand_on, name='hand_on', out_shape=out_shape, in_specs=[an...  2.76 us

profile of v5, /device:TPU:1, one launch (start us, length us, event | category | flops | bytes accessed | tf_op | source)
XLA Modules:
  0.0 99.5 jit_solution(15882677716281887810)
XLA Ops:
  0.6 96.1 %triangle.1 = (bf16[16,256,128]{2,1,0:T(8,128)(2,1)}, bf16[16,256,128]{2,1,0:T(8,128)(2,1)}, f32[6,128,128]{2,1,0:T(8,128)}) custom-call(bf16[16,256,128]{2,1,0:T(8,128)(2,1)} %bitcast.12, bf16[16,256,128]{2,1,0:T(8,128)(2,1)} %bitcast.13, bf16[128,640]{1,0:T(8,128)(2,1)} %w_in_h.3, bf16[128,128]{1,0:T(8,128)(2,1)} %w_out_h.3, f32[1,128]{1,0:T(1,128)} %bitcast.8, ...), custom_call_target="tpu_custom_call" | custom-call | flops 3300000000 | bytes 5000000 | tf_op jit(solution)/shard_map/triangle/pallas_call | solution.py:535
  96.7 2.8 %hand_on.1 = (bf16[16,256,128]{2,1,0:T(8,128)(2,1)}, bf16[16,256,128]{2,1,0:T(8,128)(2,1)}, f32[128,640]{1,0:T(8,128)}, f32[128,128]{1,0:T(8,128)}, f32[1,128]{1,0:T(1,128)}, /*index=5*/f32[1,128]{1,0:T(1,128)}) custom-call(bf16[16,256,128]{2,1,0:T(8,128)(2,1)} %get-tuple-element.15.upd_h, bf16[16,256,128]{2,1,0:T(8,128)(2,1)} %get-tuple-element.16.gpair_h, ...), custom_call_target="tpu_custom_call" | custom-call | tf_op jit(solution)/shard_map/hand_on/pallas_call | solution.py:593

commit v6 on v5

--- a/solution.py
+++ b/solution.py
@@ -64,12 +64,6 @@
             return carry
         lax.fori_loop(lo, hi, body, 0, unroll=unroll)
 
-    barrier = pltpu.get_barrier_semaphore()
-    each(1, n_ax, lambda o: pl.semaphore_signal(
-        barrier, inc=1, device_id=(dp, peer(o)), device_id_type=MESH))
-    each(1, n_dp, lambda o: pl.semaphore_signal(
-        barrier, inc=1, device_id=(dp_peer(o), me), device_id_type=MESH))
-
     half = pl.ds(0, 8), pl.ds(8, 8)
     in_pairs = {
         "w_in": (w_in_h, w_in), "gain_in": (gain_in_h, gain_in),
@@ -96,6 +90,12 @@
 
     for name in in_names:
         in_copy(name).start()
+
+    barrier = pltpu.get_barrier_semaphore()
+    for o in (10, 11, 6, 7, 14, 15, 8, 9, 2, 3, 4, 5, 12, 13, 1):
+        pl.semaphore_signal(barrier, inc=1, device_id=(dp, peer(o)), device_id_type=MESH)
+    each(1, n_dp, lambda o: pl.semaphore_signal(
+        barrier, inc=1, device_id=(dp_peer(o), me), device_id_type=MESH))
 
     def start(t):
         def one(o):

time: 99.6 us -> 99.1 us (level)
  no operation moved by 1% of the time
where the time goes in v6:
time: 99.1 us; the launch traced here: 98.9 us
  Pallas kernels  98.2 us (99%)
    pallas_call x1, Pallas kernels, local(): pl.pallas_call(functools.partial(kernel, n_dp, n_ax, factor), name='trian...  95.5 us
    pallas_call x1, Pallas kernels, local(): pl.pallas_call(hand_on, name='hand_on', out_shape=out_shape, in_specs=[an...  2.76 us

profile of v6, /device:TPU:1, one launch (start us, length us, event | category | flops | bytes accessed | tf_op | source)
XLA Modules:
  0.0 98.9 jit_solution(3383649541282120438)
XLA Ops:
  0.6 95.5 %triangle.1 = (bf16[16,256,128]{2,1,0:T(8,128)(2,1)}, bf16[16,256,128]{2,1,0:T(8,128)(2,1)}, f32[6,128,128]{2,1,0:T(8,128)}) custom-call(bf16[16,256,128]{2,1,0:T(8,128)(2,1)} %bitcast.12, bf16[16,256,128]{2,1,0:T(8,128)(2,1)} %bitcast.13, bf16[128,640]{1,0:T(8,128)(2,1)} %w_in_h.3, bf16[128,128]{1,0:T(8,128)(2,1)} %w_out_h.3, f32[1,128]{1,0:T(1,128)} %bitcast.8, ...), custom_call_target="tpu_custom_call" | custom-call | flops 3300000000 | bytes 5000000 | tf_op jit(solution)/shard_map/triangle/pallas_call | solution.py:535
  96.1 2.8 %hand_on.1 = (bf16[16,256,128]{2,1,0:T(8,128)(2,1)}, bf16[16,256,128]{2,1,0:T(8,128)(2,1)}, f32[128,640]{1,0:T(8,128)}, f32[128,128]{1,0:T(8,128)}, f32[1,128]{1,0:T(1,128)}, /*index=5*/f32[1,128]{1,0:T(1,128)}) custom-call(bf16[16,256,128]{2,1,0:T(8,128)(2,1)} %get-tuple-element.15.upd_h, bf16[16,256,128]{2,1,0:T(8,128)(2,1)} %get-tuple-element.16.gpair_h, ...), custom_call_target="tpu_custom_call" | custom-call | tf_op jit(solution)/shard_map/hand_on/pallas_call | solution.py:593

commit v7 on v6

--- a/solution.py
+++ b/solution.py
@@ -51,6 +51,7 @@
     me = lax.axis_index("axial")
     dp = lax.axis_index("dp")
     my_z, my_y, my_c = me // 4, (me // 2) % 2, me % 2
+    far_first = (10, 11, 6, 7, 14, 15, 8, 9, 2, 3, 4, 5, 12, 13, 1)
 
     def peer(o):
         return ((my_z + o // 4) % 4) * 4 + ((my_y + (o // 2) % 2) % 2) * 2 + (my_c + o % 2) % 2
@@ -92,10 +93,22 @@
         in_copy(name).start()
 
     barrier = pltpu.get_barrier_semaphore()
-    for o in (10, 11, 6, 7, 14, 15, 8, 9, 2, 3, 4, 5, 12, 13, 1):
-        pl.semaphore_signal(barrier, inc=1, device_id=(dp, peer(o)), device_id_type=MESH)
-    each(1, n_dp, lambda o: pl.semaphore_signal(
-        barrier, inc=1, device_id=(dp_peer(o), me), device_id_type=MESH))
+
+    def greet(dp_index, ax_index):
+        pl.semaphore_signal(barrier, inc=1, device_id=(dp_index, ax_index), device_id_type=MESH)
+
+    def greet_dp(o):
+        greet((dp // 4 + o // 4) % 2 * 4 + (dp % 4 + o % 4) % 4, me)
+
+    for o in far_first[:6]:
+        greet(dp, peer(o))
+    for o in (6, 5, 7, 2):
+        greet_dp(o)
+    for o in far_first[6:14]:
+        greet(dp, peer(o))
+    for o in (1, 3, 4):
+        greet_dp(o)
+    greet(dp, peer(1))
 
     def start(t):
         def one(o):
@@ -167,7 +180,8 @@
         def one(o):
             d = peer(o)
             push(dw.at[right_blocks, rows8(d)], r1.at[me], 0, dp, d)
-        each(1, n_ax, one)
+        for o in far_first:
+            one(o)
         r1[me] = dw[4:6, rows8(me)]
 
     def right_dp():
@@ -182,7 +196,8 @@
         s2[...] = jnp.sum(r2[...], axis=0) * factor
         target = fin.at[right_blocks, rows8(me)]
         pltpu.make_async_copy(s2, target, fsem.at[0]).start()
-        each(1, n_ax, lambda o: push(s2, target, 2, dp, peer(o)))
+        for o in far_first:
+            push(s2, target, 2, dp, peer(o))
 
     my_x, my_yl = dp % 4, dp // 4
 

time: 99.1 us -> 98.8 us (level)
  no operation moved by 1% of the time
where the time goes in v7:
time: 98.8 us; the launch traced here: 98.6 us
  Pallas kernels  97.9 us (99%)
    pallas_call x1, Pallas kernels, local(): pl.pallas_call(functools.partial(kernel, n_dp, n_ax, factor), name='trian...  95.2 us
    pallas_call x1, Pallas kernels, local(): pl.pallas_call(hand_on, name='hand_on', out_shape=out_shape, in_specs=[an...  2.76 us

profile of v7, /device:TPU:1, one launch (start us, length us, event | category | flops | bytes accessed | tf_op | source)
XLA Modules:
  0.0 98.6 jit_solution(15736530704798128660)
XLA Ops:
  0.6 95.2 %triangle.1 = (bf16[16,256,128]{2,1,0:T(8,128)(2,1)}, bf16[16,256,128]{2,1,0:T(8,128)(2,1)}, f32[6,128,128]{2,1,0:T(8,128)}) custom-call(bf16[16,256,128]{2,1,0:T(8,128)(2,1)} %bitcast.12, bf16[16,256,128]{2,1,0:T(8,128)(2,1)} %bitcast.13, bf16[128,640]{1,0:T(8,128)(2,1)} %w_in_h.3, bf16[128,128]{1,0:T(8,128)(2,1)} %w_out_h.3, f32[1,128]{1,0:T(1,128)} %bitcast.8, ...), custom_call_target="tpu_custom_call" | custom-call | flops 3300000000 | bytes 5000000 | tf_op jit(solution)/shard_map/triangle/pallas_call | solution.py:550
  95.8 2.8 %hand_on.1 = (bf16[16,256,128]{2,1,0:T(8,128)(2,1)}, bf16[16,256,128]{2,1,0:T(8,128)(2,1)}, f32[128,640]{1,0:T(8,128)}, f32[128,128]{1,0:T(8,128)}, f32[1,128]{1,0:T(1,128)}, /*index=5*/f32[1,128]{1,0:T(1,128)}) custom-call(bf16[16,256,128]{2,1,0:T(8,128)(2,1)} %get-tuple-element.15.upd_h, bf16[16,256,128]{2,1,0:T(8,128)(2,1)} %get-tuple-element.16.gpair_h, ...), custom_call_target="tpu_custom_call" | custom-call | tf_op jit(solution)/shard_map/hand_on/pallas_call | solution.py:608
